TPU v7x, 32 devices: a whole 2x2x4 slice. The times are simulated.
32 devices in a mesh: req: 8 (over y, x, core), tensor: 4 (over z).
Axes of the slice: x: 2, y: 2, z: 4, core: 2. Of those that a mesh axis runs over, the one named last changes fastest.
Arguments:
- hidden: bfloat16 [16, 512, 1792], P('req', 'tensor')
- suffix_len: int32 [16], P('req'), may hold values from 1 to 512, as said below
- request_group: int32 [16], P('req'), may hold values from 0 to 31
- group_slot: int32 [32], replicated, may hold values from 0 to 31, each once
- norm_first: float32 [1792], replicated, may hold values from 0.5 to 2
- query_weight: bfloat16 [1792, 256], P(None, 'tensor'), may hold values from -0.125 to 0.125
- key_weight: bfloat16 [1792, 256], P(None, 'tensor'), may hold values from -0.125 to 0.125
- value_weight: bfloat16 [1792, 1792], P(None, 'tensor'), may hold values from -0.125 to 0.125
- filter_gate: bfloat16 [1792, 1792], P(None, 'tensor'), may hold values from -0.125 to 0.125
- filter_taps: float32 [3, 1792], P(None, 'tensor'), may hold values from -3 to 3
- linear_out: bfloat16 [1792, 1792], P('tensor'), may hold values from -0.125 to 0.125
- norm_second: float32 [1792], replicated, may hold values from 0.5 to 1.5
- window_query: bfloat16 [1792, 1792], P(None, 'tensor')
- window_key: bfloat16 [1792, 1792], P(None, 'tensor')
- window_value: bfloat16 [1792, 1792], P(None, 'tensor'), may hold values from -0.125 to 0.125
- window_out: bfloat16 [1792, 1792], P('tensor'), may hold values from -0.125 to 0.125
- norm_third: float32 [1792], replicated, may hold values from 0.5 to 1.5
- gate_weight: bfloat16 [1792, 7168], P(None, 'tensor'), may hold values from -0.125 to 0.125
- up_weight: bfloat16 [1792, 7168], P(None, 'tensor'), may hold values from -0.125 to 0.125
- down_weight: bfloat16 [7168, 1792], P('tensor'), may hold values from -0.0625 to 0.0625
- prefix_sums: float32 [32, 16, 273, 112], P('req', 'tensor'), as said below
- prefix_norms: float32 [32, 16, 273], P('req', 'tensor'), as said below
- prefix_keys: bfloat16 [32, 64, 1792], P('req', None, 'tensor'), may hold values from -6 to 6
- prefix_values: bfloat16 [32, 64, 1792], P('req', None, 'tensor'), may hold values from -6 to 6
- prefix_tail: bfloat16 [32, 2, 1792], P('req', None, 'tensor'), may hold values from -10 to 10
Outputs:
- hidden_out: bfloat16 [16, 512, 1792], P('req', 'tensor')
- final_norm: float32 [16], P('req')
- top_logit: float32 [16], P('req')
Inputs may be any that keep to these rules, and one draw needn't show every extreme that they name: `suffix_len`: each request's suffix is either a short one of at most 32 tokens or a long one of more than 384; some request has exactly 512. `group_slot`: each slot holds exactly one group. `prefix_sums`: A sum over 128 prefix tokens of the key feature map times the value. `prefix_norms`: A sum over the same 128 tokens of the key feature map, so its inner product with any feature map is positive.
All inputs are finite; a program needn't handle non-finite values.
Results may differ from a plain program's by a relative error of at most 0.024.
Values may be sent and summed in bfloat16 or wider, within the bound.
No kernel may reach another device: no remote copies, remote signals or barrier semaphores. Data moves between devices by JAX's collectives and lax.ppermute only.
A program may use at most 128 MiB of HBM per device.

v0:
```python
import jax
import jax.numpy as jnp
from jax import lax
from jax.sharding import PartitionSpec as P

D = 1792
FD = 16
HS = 112
WIN = 64
KC = 3
LMAX = 512


EPS = 1e-05


def rms_norm(row_block, gain_vector):
    floats = row_block.astype(jnp.float32)
    inverse_rms = lax.rsqrt(jnp.mean(floats * floats, axis=-1, keepdims=True) + EPS)
    return (floats * inverse_rms * gain_vector).astype(jnp.bfloat16)


def features(vectors):
    floats = vectors.astype(jnp.float32)
    dimension = floats.shape[-1]
    constant = jnp.ones(floats.shape[:-1] + (1,), jnp.float32)
    linear_part = floats * dimension ** (-0.25)
    square_part = (floats[..., :, None] * floats[..., None, :]).reshape(
        floats.shape[:-1] + (dimension * dimension,)
    )
    square_part = square_part * (2.0 * dimension) ** (-0.5)
    return jnp.concatenate([constant, linear_part, square_part], axis=-1)


def slot_lookup(groups, group_slot):
    matches = jnp.arange(group_slot.shape[0])[None, :] == groups[:, None]
    return jnp.sum(jnp.where(matches, group_slot[None, :], 0), axis=1)


def per_device(
    hidden,
    suffix_len,
    request_group,
    group_slot,
    norm_first,
    query_weight,
    key_weight,
    value_weight,
    filter_gate,
    filter_taps,
    linear_out,
    norm_second,
    window_query,
    window_key,
    window_value,
    window_out,
    norm_third,
    gate_weight,
    up_weight,
    down_weight,
    prefix_sums,
    prefix_norms,
    prefix_keys,
    prefix_values,
    prefix_tail,
):
    requests_here = hidden.shape[0]
    share_rows = hidden.shape[1]
    model_width = hidden.shape[2]
    lin_heads = prefix_sums.shape[1]
    win_heads = prefix_keys.shape[2] // HS
    slot_ids = slot_lookup(request_group, group_slot)
    all_sums, all_norms = (
        lax.all_gather(prefix_sums.astype(jnp.bfloat16), "req", axis=0, tiled=True).astype(
            prefix_sums.dtype
        ),
        lax.all_gather(prefix_norms.astype(jnp.bfloat16), "req", axis=0, tiled=True).astype(
            prefix_norms.dtype
        ),
    )
    all_keys, all_values, all_tails = (
        lax.all_gather(prefix_keys, "req", axis=0, tiled=True),
        lax.all_gather(prefix_values, "req", axis=0, tiled=True),
        lax.all_gather(prefix_tail, "req", axis=0, tiled=True),
    )
    picked_sum = jnp.take(all_sums, slot_ids, axis=0)
    picked_norm = jnp.take(all_norms, slot_ids, axis=0)
    picked_keys = jnp.take(all_keys, slot_ids, axis=0)
    picked_values = jnp.take(all_values, slot_ids, axis=0)
    picked_tail = jnp.take(all_tails, slot_ids, axis=0)

    def settle(stream, partial_sum, gain_vector):
        summed = lax.psum(partial_sum.astype(jnp.bfloat16), "tensor").astype(jnp.float32)
        stream = (stream.astype(jnp.float32) + summed).astype(jnp.bfloat16)
        normed = None if gain_vector is None else rms_norm(stream, gain_vector)
        return (stream, normed)

    stream = lax.all_gather(hidden, "tensor", axis=1, tiled=True)
    normed = rms_norm(stream, norm_first)
    position = jnp.arange(LMAX)
    causal = position[:, None] >= position[None, :]
    key_place = jnp.arange(WIN + LMAX)
    allowed = (key_place[None, :] > position[:, None]) & (
        key_place[None, :] <= position[:, None] + WIN
    )

    def project(normed_rows, matrix):
        flat_rows = normed_rows.reshape(requests_here * LMAX, model_width)
        return jnp.dot(flat_rows, matrix, preferred_element_type=jnp.float32).astype(jnp.bfloat16)

    queries = project(normed, query_weight).reshape(requests_here, LMAX, lin_heads, FD)
    key_rows = project(normed, key_weight).reshape(requests_here, LMAX, lin_heads, FD)
    values_lin = project(normed, value_weight).reshape(requests_here, LMAX, lin_heads * HS)
    gating = project(normed, filter_gate).reshape(requests_here, LMAX, lin_heads * HS)
    extended = jnp.concatenate([picked_tail, values_lin], axis=1).astype(jnp.float32)
    convolved = sum(
        (
            filter_taps[offset] * extended[:, KC - 1 - offset : KC - 1 - offset + LMAX]
            for offset in range(KC)
        )
    )
    mixed_values = (
        (convolved * jax.nn.silu(gating.astype(jnp.float32)))
        .astype(jnp.bfloat16)
        .reshape(requests_here, LMAX, lin_heads, HS)
    )
    scores = jnp.einsum(
        "rthf,rshf->rhts", queries, key_rows, preferred_element_type=jnp.float32
    ) * FD ** (-0.5)
    weights_lin = jnp.where(causal, 1.0 + scores + 0.5 * scores * scores, 0.0)
    numerator = jnp.einsum(
        "rhts,rshd->rthd",
        weights_lin.astype(jnp.bfloat16),
        mixed_values,
        preferred_element_type=jnp.float32,
    )
    denominator = jnp.transpose(jnp.sum(weights_lin, axis=-1), (0, 2, 1))
    mapped = features(queries)
    numerator = numerator + jnp.einsum(
        "rthf,rhfd->rthd", mapped, picked_sum, precision=lax.Precision.HIGHEST
    )
    denominator = denominator + jnp.einsum(
        "rthf,rhf->rth", mapped, picked_norm, precision=lax.Precision.HIGHEST
    )
    linear_rows = (
        (numerator / denominator[..., None])
        .astype(jnp.bfloat16)
        .reshape(requests_here * LMAX, lin_heads * HS)
    )
    partial_sum = jnp.dot(linear_rows, linear_out, preferred_element_type=jnp.float32).reshape(
        requests_here, LMAX, model_width
    )
    stream, normed = settle(stream, partial_sum, norm_second)
    window_q = project(normed, window_query).reshape(requests_here, LMAX, win_heads, HS)
    window_k = project(normed, window_key).reshape(requests_here, LMAX, win_heads * HS)
    window_v = project(normed, window_value).reshape(requests_here, LMAX, win_heads * HS)
    all_keys = jnp.concatenate([picked_keys, window_k], axis=1).reshape(
        requests_here, WIN + LMAX, win_heads, HS
    )
    all_values = jnp.concatenate([picked_values, window_v], axis=1).reshape(
        requests_here, WIN + LMAX, win_heads, HS
    )
    logits = jnp.einsum(
        "rthd,rphd->rhtp", window_q, all_keys, preferred_element_type=jnp.float32
    ) * HS ** (-0.5)
    logits = jnp.where(allowed, logits, -jnp.inf)
    row_max = jnp.max(logits, axis=-1, keepdims=True)
    exponent = jnp.exp(logits - row_max)
    probabilities = (exponent / jnp.sum(exponent, axis=-1, keepdims=True)).astype(jnp.bfloat16)
    attended = jnp.einsum(
        "rhtp,rphd->rthd", probabilities, all_values, preferred_element_type=jnp.float32
    ).astype(jnp.bfloat16)
    attended = attended.reshape(requests_here * LMAX, win_heads * HS)
    final_whole = position[None, :] == suffix_len[:, None] - 1
    local_top = jnp.max(jnp.where(final_whole[:, None, :], row_max[..., 0], -jnp.inf), axis=(1, 2))
    partial_sum = jnp.dot(attended, window_out, preferred_element_type=jnp.float32).reshape(
        requests_here, LMAX, model_width
    )
    stream, normed = settle(stream, partial_sum, norm_third)
    flat_rows = normed.reshape(requests_here * LMAX, model_width)
    gate_rows = jnp.dot(flat_rows, gate_weight, preferred_element_type=jnp.float32)
    up_rows = jnp.dot(flat_rows, up_weight, preferred_element_type=jnp.float32)
    inner_rows = (jax.nn.silu(gate_rows) * up_rows).astype(jnp.bfloat16)
    partial_sum = jnp.dot(inner_rows, down_weight, preferred_element_type=jnp.float32).reshape(
        requests_here, LMAX, model_width
    )
    stream, unused = settle(stream, partial_sum, None)
    row_start = lax.axis_index("tensor") * share_rows
    stream = lax.dynamic_slice_in_dim(stream, row_start, share_rows, 1)
    rows_here = row_start + jnp.arange(share_rows)
    valid = rows_here[None, :] < suffix_len[:, None]
    hidden_out = jnp.where(valid[..., None], stream, jnp.zeros_like(stream))
    stream_f = stream.astype(jnp.float32)
    live_term = jnp.sum(jnp.where(valid[..., None], stream_f * stream_f, 0.0), axis=(1, 2))
    squares = lax.psum(live_term, "tensor")
    top_logit = lax.pmax(local_top, "tensor")
    return (hidden_out, jnp.sqrt(squares / D), top_logit)


def solution(mesh):
    return jax.shard_map(
        per_device,
        mesh=mesh,
        in_specs=(
            P("req", "tensor", None),
            P("req"),
            P("req"),
            P(),
            P(),
            P(None, "tensor"),
            P(None, "tensor"),
            P(None, "tensor"),
            P(None, "tensor"),
            P(None, "tensor"),
            P("tensor", None),
            P(),
            P(None, "tensor"),
            P(None, "tensor"),
            P(None, "tensor"),
            P("tensor", None),
            P(),
            P(None, "tensor"),
            P(None, "tensor"),
            P("tensor", None),
            P("req", "tensor", None, None),
            P("req", "tensor", None),
            P("req", None, "tensor"),
            P("req", None, "tensor"),
            P("req", None, "tensor"),
        ),
        out_specs=(P("req", "tensor", None), P("req"), P("req")),
        check_vma=False,
    )
```

profile of v0, /device:TPU:0, one launch (start us, length us, event | category | flops | bytes accessed | tf_op | source)
XLA Modules:
  0.0 717.9 jit_solution(17490503389304569684)
XLA Ops:
  8.0 3.0 convert_element_type.139
  12.8 10.7 %all_gather.21 = bf16[32,4,273]{2,1,0:T(4,128)(2,1)S(1)} all-gather(bf16[4,4,273]{2,1,0:T(4,128)(2,1)S(1)} %convert_element_type.142), channel_id=1, replica_groups=mesh['req'=8,'tensor'=4] {'req'}, dimensions={0}, use_global_device_ids=true | all-gather | bytes 78624 | tf_op jit(solution)/shard_map/all_gather | solution.py:77
  23.5 9.2 %all_gather.19 = bf16[32,2,448]{2,1,0:T(2,128)(2,1)S(1)} all-gather(bf16[4,2,448]{2,1,0:T(2,128)(2,1)S(1)} %copy-done.16), channel_id=1, replica_groups=mesh['req'=8,'tensor'=4] {'req'}, dimensions={0}, use_global_device_ids=true | all-gather | bytes 64512 | tf_op jit(solution)/shard_map/all_gather | solution.py:84
  34.2 50.2 %all-gather.5.cloned.1.call-done = bf16[2,512,1792]{2,1,0:T(8,128)(2,1)} async-done(((bf16[2,128,1792]{2,1,0:T(8,128)(2,1)}), bf16[2,512,1792]{2,1,0:T(8,128)(2,1)}) %all-gather.5.cloned.1.call-update) | async-done | bytes 3670032 | tf_op jit(solution)/shard_map/all_gather | solution.py:98
  84.5 3.0 fusion.1
  91.7 2.8 multiply_multiply_fusion
  97.6 4.4 convolution_convert_fusion.7
  102.1 2.8 fusion.10
  105.0 2.9 fusion.17
  112.0 3.2 fusion.13
  115.3 26.5 %all-gather.7.cloned.1.call-done = bf16[32,4,273,112]{3,1,2,0:T(4,128)(2,1)} async-done(((bf16[4,4,273,112]{3,1,2,0:T(4,128)(2,1)}), bf16[32,4,273,112]{3,1,2,0:T(4,128)(2,1)}) %all-gather.7.cloned.1.call-update) | async-done | bytes 7827472 | tf_op jit(solution)/shard_map/all_gather | solution.py:74
  141.8 9.6 %convert_element_type.140 = f32[32,4,273,112]{3,1,2,0:T(4,128)} convert(bf16[32,4,273,112]{3,1,2,0:T(4,128)(2,1)} %all-gather.7.cloned.1.call-done) | non-fusion elementwise | flops 3913728 | bytes 23482368 | tf_op jit(solution)/shard_map/convert_element_type | solution.py:74
  151.4 7.3 %gather_fusion.1 = f32[2,4,273,112]{3,1,2,0:T(4,128)S(1)} fusion(f32[32,4,273,112]{3,1,2,0:T(4,128)} %convert_element_type.140, s32[1024]{0:T(1024)S(1)} %pad_clamp_fusion.1), kind=kCustom, calls=%fused_computation.3 | custom fusion | bytes 1956872 | tf_op jit(solution)/shard_map/jit(_take)/gather | solution.py:86
  159.0 7.0 fusion.29
  166.0 4.0 convolution_convert_fusion.2
  173.7 27.5 %all-gather.11.cloned.1.call-done = bf16[32,64,448]{2,1,0:T(8,128)(2,1)} async-done(((bf16[4,64,448]{2,1,0:T(8,128)(2,1)}), bf16[32,64,448]{2,1,0:T(8,128)(2,1)}) %all-gather.11.cloned.1.call-update) | async-done | bytes 1835024 | tf_op jit(solution)/shard_map/all_gather | solution.py:82
  204.5 137.1 %all-reduce.4.cloned.1.call-done = bf16[2,512,1792]{2,1,0:T(8,128)(2,1)} async-done(((bf16[2,512,1792]{2,1,0:T(8,128)(2,1)}), bf16[2,512,1792]{2,1,0:T(8,128)(2,1)}) %all-reduce.4.cloned.1.call-update) | async-done | bytes 3670032 | tf_op jit(solution)/shard_map/psum | solution.py:93
  341.6 4.5 fusion.5
  352.5 4.4 convolution_convert_fusion.4
  357.6 5.3 convolution_convert_fusion.5
  362.9 3.0 concatenate.25
  366.0 3.4 fusion
  371.3 3.4 fusion.32
  374.8 3.9 convolution_convert_fusion.1
  379.0 136.9 %all-reduce.6.cloned.1.call-done = bf16[2,512,1792]{2,1,0:T(8,128)(2,1)} async-done(((bf16[2,512,1792]{2,1,0:T(8,128)(2,1)}), bf16[2,512,1792]{2,1,0:T(8,128)(2,1)}) %all-reduce.6.cloned.1.call-update) | async-done | bytes 3670032 | tf_op jit(solution)/shard_map/psum | solution.py:93
  515.9 7.4 %fusion.16 = (f32[2,512,1792]{2,1,0:T(8,128)}, f32[2,512]{1,0:T(2,128)S(1)}) fusion(bf16[2,512,1792]{2,1,0:T(8,128)(2,1)} %all-reduce.6.cloned.1.call-done, bf16[2,512,1792]{2,1,0:T(8,128)(2,1)} %copy-done.5), kind=kLoop, calls=%fused_computation.38 | loop fusion | flops 12844032 | bytes 14684160 | tf_op jit(solution)/shard_map/convert_element_type | solution.py:94
  526.6 11.7 %fusion.64 = f32[1024,1792]{1,0:T(8,128)} fusion(bf16[1024,1792]{1,0:T(8,128)(2,1)S(1)} %bitcast.109, bf16[1792,1792]{1,0:T(8,128)(2,1)} %param.44), kind=kOutput, calls=%fused_computation.129 | convolution fusion | flops 6576668672 | bytes 17432576 | tf_op jit(solution)/shard_map/dot_general | solution.py:181
  538.2 21.7 %convolution_convert_fusion = bf16[1024,1792]{1,0:T(8,128)(2,1)} fusion(bf16[1792,1792]{1,0:T(8,128)(2,1)} %param.46, f32[1024,1792]{1,0:T(8,128)} %fusion.64, bf16[1024,1792]{1,0:T(8,128)(2,1)} %bitcast.110, bf16[1792,1792]{1,0:T(8,128)(2,1)} %param.45), kind=kOutput, calls=%fused_computation.35 | convolution fusion | flops 13166182400 | bytes 27525120 | tf_op jit(solution)/shard_map/dot_general | solution.py:184
  560.9 10.1 %pmax.7 = f32[2]{0:T(128)} all-reduce(f32[2]{0:T(128)S(1)} %select_reduce_fusion.1), channel_id=1, replica_groups=mesh['req'=8,'tensor'=4] {'tensor'}, use_global_device_ids=true, to_apply=%region_13.15 | all-reduce | flops 2 | bytes 16 | tf_op jit(solution)/shard_map/pmax | solution.py:196
  570.9 126.3 %all-reduce.8.cloned.1.call-done = bf16[2,512,1792]{2,1,0:T(8,128)(2,1)} async-done(((bf16[2,512,1792]{2,1,0:T(8,128)(2,1)}), bf16[2,512,1792]{2,1,0:T(8,128)(2,1)}) %all-reduce.8.cloned.1.call-update) | async-done | bytes 3670032 | tf_op jit(solution)/shard_map/psum | solution.py:93
  697.3 2.3 select_reduce_fusion
  700.7 9.4 %psum.31 = f32[2]{0:T(128)S(1)} all-reduce(f32[2]{0:T(128)S(1)} %get-tuple-element.4), channel_id=1, replica_groups=mesh['req'=8,'tensor'=4] {'tensor'}, use_global_device_ids=true, to_apply=%region_11.13 | all-reduce | flops 2 | bytes 16 | tf_op jit(solution)/shard_map/psum | solution.py:195
  (123 shorter events, 37.8 us)
Async XLA Ops:
  7.2 158.8 %copy-start = (bf16[448,1792]{1,0:T(8,128)(2,1)S(1)}, bf16[448,1792]{1,0:T(8,128)(2,1)}, u32[]{:S(2)}) copy-start(bf16[448,1792]{1,0:T(8,128)(2,1)} %param.37) | copy-start | bytes 4816900
  7.2 5.2 copy-start.25
  7.2 5.2 copy-start.24
  7.2 5.6 copy-start.15
  7.2 16.3 %copy-start.16 = (bf16[4,2,448]{2,1,0:T(2,128)(2,1)S(1)}, bf16[4,2,448]{2,1,0:T(2,128)(2,1)}, u32[]{:S(2)}) copy-start(bf16[4,2,448]{2,1,0:T(2,128)(2,1)} %param.51) | copy-start | bytes 21508
  7.2 27.0 %copy-start.20 = (f32[3,448]{1,0:T(4,128)S(1)}, f32[3,448]{1,0:T(4,128)}, u32[]{:S(2)}) copy-start(f32[3,448]{1,0:T(4,128)} %param.36) | copy-start | bytes 16132
  7.2 77.2 %all-gather.5.cloned.1.call-start = ((), (), s32[]{:S(2)}) async-start(), calls=%async_computation | async-start | bytes 4587520 | tf_op jit(solution)/shard_map/all_gather | solution.py:98
  8.0 133.8 %all-gather.7.cloned.1.call-start = ((), (), s32[]{:S(2)}) async-start(), calls=%async_computation.1 | async-start | bytes 10063872 | tf_op jit(solution)/shard_map/all_gather | solution.py:74
  11.0 76.4 %copy-start.17 = (f32[1792]{0:T(1024)S(1)}, f32[1792]{0:T(1024)}, u32[]{:S(2)}) copy-start(f32[1792]{0:T(1024)} %param.31) | copy-start | bytes 21508
  11.1 160.5 %all-gather.9.cloned.1.call-start = ((), (), s32[]{:S(2)}) async-start(), calls=%async_computation.3 | async-start | bytes 2359296 | tf_op jit(solution)/shard_map/all_gather | solution.py:83
  11.8 189.4 %all-gather.11.cloned.1.call-start = ((), (), s32[]{:S(2)}) async-start(), calls=%async_computation.4 | async-start | bytes 2359296 | tf_op jit(solution)/shard_map/all_gather | solution.py:82
  12.4 329.2 %all-reduce.4.cloned.1.call-start = ((), (), s32[]{:S(2)}) async-start(), calls=%async_computation.2 | async-start | bytes 7340032 | tf_op jit(solution)/shard_map/psum | solution.py:93
  84.5 3.1 copy-start.7
  87.6 2.7 copy-start.12
  88.5 1.8 copy-start.2
  91.6 3.0 copy-start.13
  91.7 4.0 copy-start.3
  97.6 4.5 copy-start.14
  102.1 2.9 copy-start.8
  104.9 3.4 copy-start.4
  105.0 3.4 copy-start.21
  169.9 346.0 %all-reduce.6.cloned.1.call-start = ((), (), s32[]{:S(2)}) async-start(), calls=%async_computation.5 | async-start | bytes 7340032 | tf_op jit(solution)/shard_map/psum | solution.py:93
  204.5 141.6 %copy-start.18 = (f32[1792]{0:T(1024)S(1)}, f32[1792]{0:T(1024)}, u32[]{:S(2)}) copy-start(f32[1792]{0:T(1024)} %param.38) | copy-start | bytes 21508
  346.1 1.9 copy-start.5
  346.1 3.7 copy-start.22
  371.3 3.4 copy-start.23
  378.7 144.6 %copy-start.19 = (f32[1792]{0:T(1024)S(1)}, f32[1792]{0:T(1024)}, u32[]{:S(2)}) copy-start(f32[1792]{0:T(1024)} %param.43) | copy-start | bytes 21508
  378.7 318.5 %all-reduce.8.cloned.1.call-start = ((), (), s32[]{:S(2)}) async-start(), calls=%async_computation.6 | async-start | bytes 7340032 | tf_op jit(solution)/shard_map/psum | solution.py:93
  515.9 7.4 %copy-start.6 = (bf16[2,512,1792]{2,1,0:T(8,128)(2,1)S(1)}, bf16[2,512,1792]{2,1,0:T(8,128)(2,1)}, u32[]{:S(2)}) copy-start(bf16[2,512,1792]{2,1,0:T(8,128)(2,1)} %copy-done.5) | copy-start | bytes 11010052
  515.9 7.4 %copy-start.9 = (bf16[2,512,1792]{2,1,0:T(8,128)(2,1)S(1)}, bf16[2,512,1792]{2,1,0:T(8,128)(2,1)}, u32[]{:S(2)}) copy-start(bf16[2,512,1792]{2,1,0:T(8,128)(2,1)} %all-reduce.6.cloned.1.call-done) | copy-start | bytes 11010052
  524.7 1.8 copy-start.11
  560.0 150.6 %copy-start.1 = (bf16[448,1792]{1,0:T(8,128)(2,1)S(1)}, bf16[448,1792]{1,0:T(8,128)(2,1)}, u32[]{:S(2)}) copy-start(bf16[448,1792]{1,0:T(8,128)(2,1)} %param.37) | copy-start | bytes 4816900
  (2 other events, 2.5 us)
Sparse Core Ops, SparseCore 0:
  9.6 74.7 all-gather.4
  86.4 55.3 all-gather.6
  143.7 27.8 all-gather.8
  173.3 27.8 all-gather.10
  203.5 138.0 all-reduce.3
  378.8 137.0 all-reduce.5
  560.1 137.1 all-reduce.7
where the time goes:
time: 728 us; the launch traced here: 718 us
  waiting for transfers between devices  508 us (70%)
  matrix products  84.7 us (12%)
  other arithmetic  42.6 us (6%)
  blocking collectives  39.4 us (5%)
  local copies, waits for them, and re-layouts  27.7 us (4%)
  between operations  15.1 us (2%)
    psum x3, waiting for transfers between devices, settle(): lax.psum(partial_sum.astype(jnp.bfloat16), 'tensor').astype(jnp.float32)  400 us
    all_gather x1, waiting for transfers between devices, per_device(): stream = lax.all_gather(hidden, 'tensor', axis=1, tiled=True)  50.2 us
    all_gather x1, waiting for transfers between devices, per_device(): lax.all_gather(prefix_keys, 'req', axis=0, tiled=True)  27.5 us
    all_gather x1, waiting for transfers between devices, per_device(): lax.all_gather(prefix_sums.astype(jnp.bfloat16), 'req', axis=0, tiled=True)  26.5 us
    dot_general x1, matrix products, per_device(): jnp.dot(inner_rows, down_weight, preferred_element_type=jnp.float32)  21.7 us
    dot_general x7, matrix products, project(): jnp.dot(flat_rows, matrix, preferred_element_type=jnp.float32)  20.7 us
  transfers between devices with their start and end apart: 7, of which 7 were waited for; matrix products, arithmetic and copies ran while one was open for 9% of the time, Pallas kernels for 0%

commit v1 on v0

v1 whole, which is shorter than its diff:
```python
import jax
import jax.numpy as jnp
from jax import lax
from jax.sharding import PartitionSpec as P

D = 1792
FD = 16
HS = 112
WIN = 64
KC = 3
LMAX = 512
PAIRS = FD // 2 + 1

EPS = 1e-05
BF = jnp.bfloat16
F32 = jnp.float32


def rms_norm(rows, gain):
    floats = rows.astype(F32)
    inverse_rms = lax.rsqrt(jnp.mean(floats * floats, axis=-1, keepdims=True) + EPS)
    return (floats * inverse_rms * gain).astype(BF)


def dot(left, right):
    return jnp.dot(left, right, preferred_element_type=F32)


def folded_features(queries):
    floats = jnp.transpose(queries.astype(F32), (1, 0, 2))
    parts = [jnp.ones(floats.shape[:-1] + (1,), F32), floats * FD ** (-0.25)]
    for shift in range(PAIRS):
        parts.append(floats * jnp.roll(floats, -shift, axis=-1) * (2.0 * FD) ** (-0.5))
    return jnp.concatenate(parts, axis=-1)


def fold_matrix():
    row = jnp.arange(1 + FD + PAIRS * FD)[:, None]
    column = jnp.arange(1 + FD + FD * FD)[None, :]
    shift, first = (row - 1 - FD) // FD, (row - 1 - FD) % FD
    second = (first + shift) % FD
    major, minor = (column - 1 - FD) // FD, (column - 1 - FD) % FD
    straight = (major == first) & (minor == second)
    swapped = (major == second) & (minor == first) & (shift > 0) & (shift < FD // 2)
    squares = (row > FD) & (column > FD) & (straight | swapped)
    return jnp.where((row == column) & (row <= FD) | squares, 1.0, 0.0).astype(F32)


def line_gather(rows, axis, count):
    here = lax.axis_index(axis)
    size = rows.shape[0]
    up = down = rows
    ups, downs = [], []
    for step in range(1, count):
        up = lax.ppermute(up, axis, [(i, i + 1) for i in range(step - 1, count - 1)])
        down = lax.ppermute(down, axis, [(i + 1, i) for i in range(count - step)])
        ups.append(up)
        downs.append(down)
    around = jnp.concatenate(ups[::-1] + [rows] + downs)
    return lax.dynamic_slice_in_dim(around, (count - 1 - here) * size, count * size, 0)


def line_scatter(partial, axis, count):
    here = lax.axis_index(axis)
    size = partial.shape[0] // count

    def block(index):
        return lax.dynamic_slice_in_dim(partial, index * size, size, 0)

    up = down = None
    for step in range(1, count):
        to_up = block(jnp.minimum(here + count - step, count - 1))
        to_down = block(jnp.maximum(here - count + step, 0))
        if up is not None:
            to_up, to_down = to_up + up, to_down + down
        up = lax.ppermute(to_up, axis, [(i, i + 1) for i in range(step)])
        down = lax.ppermute(to_down, axis, [(i + 1, i) for i in range(count - 1 - step, count - 1)])
    return block(here).astype(F32) + up.astype(F32) + down.astype(F32)


def middle_exchange(partial, stream, axis):
    here = lax.axis_index(axis)
    half = partial.shape[0] // 2
    low = here < 2
    middle = (here == 1) | (here == 2)

    def near_far(rows):
        first, second = rows[:half], rows[half:]
        return jnp.where(low, first, second), jnp.where(low, second, first)

    inward, across, outward = [(0, 1), (3, 2)], [(1, 2), (2, 1)], [(1, 0), (2, 3)]
    near, far = near_far(partial)
    far_in = lax.ppermute(far, axis, inward)
    near_in = lax.ppermute(near, axis, inward)
    crossed = lax.ppermute(far + far_in, axis, across)
    total = near.astype(F32) + near_in.astype(F32) + crossed.astype(F32)
    own = (near_far(stream)[0].astype(F32) + total).astype(BF)
    other = lax.ppermute(own, axis, across)
    own_out = lax.ppermute(own, axis, outward)
    other_out = lax.ppermute(other, axis, outward)
    near = jnp.where(middle, own, own_out)
    far = jnp.where(middle, other, other_out)
    return jnp.concatenate([jnp.where(low, near, far), jnp.where(low, far, near)])


def settle(partial, stream, axis, count):
    if count == 4:
        return middle_exchange(partial, stream, axis)
    here = lax.axis_index(axis)
    size = partial.shape[0] // count
    mine = lax.dynamic_slice_in_dim(stream, here * size, size, 0)
    total = line_scatter(partial, axis, count)
    return line_gather((mine.astype(F32) + total).astype(BF), axis, count)


def bring_home(packs, axis, count):
    here = lax.axis_index(axis)
    bit = 1
    while bit < count:
        pairs = packs.reshape((packs.shape[0] // 2, 2) + packs.shape[1:])
        upper = (here & bit) != 0
        keep = jnp.where(upper, pairs[:, 1], pairs[:, 0])
        send = jnp.where(upper, pairs[:, 0], pairs[:, 1])
        packs = keep + lax.ppermute(send, axis, [(i, i ^ bit) for i in range(count)])
        bit *= 2
    return packs[0]


def make(req_count, tensor_count):
    def per_device(
        hidden,
        suffix_len,
        request_group,
        group_slot,
        norm_first,
        query_weight,
        key_weight,
        value_weight,
        filter_gate,
        filter_taps,
        linear_out,
        norm_second,
        window_query,
        window_key,
        window_value,
        window_out,
        norm_third,
        gate_weight,
        up_weight,
        down_weight,
        prefix_sums,
        prefix_norms,
        prefix_keys,
        prefix_values,
        prefix_tail,
    ):
        requests_here = hidden.shape[0]
        share_rows = hidden.shape[1]
        slots_here, heads = prefix_sums.shape[:2]
        width = heads * HS

        groups = lax.all_gather(request_group, "req", axis=0, tiled=True)
        matches = jnp.arange(group_slot.shape[0])[None, :] == groups[:, None]
        slots = jnp.sum(jnp.where(matches, group_slot[None, :], 0), axis=1)
        fold = fold_matrix()
        sums = jnp.einsum("fg,ahgd->afhd", fold, prefix_sums, precision=lax.Precision.HIGHEST)
        terms = sums.shape[1]
        norms = jnp.einsum("fg,ahg->afh", fold, prefix_norms, precision=lax.Precision.HIGHEST)
        norms = jnp.pad(norms.reshape(slots_here, -1), ((0, 0), (0, 2 * width - terms * heads)))
        pack = jnp.concatenate(
            [
                sums.reshape(slots_here, terms, width).astype(BF),
                norms.reshape(slots_here, 2, width).astype(BF),
                prefix_keys,
                prefix_values,
                prefix_tail,
            ],
            axis=1,
        )
        rows = pack.shape[1]
        pack = jnp.pad(pack, ((0, 0), (0, -rows % 32), (0, 0)))
        half = pack.shape[1] // 2
        pack = jnp.concatenate([pack[:, :half], pack[:, half:]], axis=2)
        local = slots - lax.axis_index("req") * slots_here
        owned = (local >= 0) & (local < slots_here)
        sent = jnp.take(pack, jnp.clip(local, 0, slots_here - 1), axis=0)
        sent = jnp.where(owned[:, None, None], sent, jnp.zeros_like(sent))
        sent = sent.reshape((req_count, requests_here) + sent.shape[1:])
        states = bring_home(sent, "req", req_count)
        states = jnp.concatenate([states[:, :, :width], states[:, :, width:]], axis=1)

        position = jnp.arange(LMAX)
        causal = position[:, None] >= position[None, :]
        bands = LMAX // WIN
        band_row = jnp.arange(WIN)[:, None]
        band_key = jnp.arange(2 * WIN)[None, :]
        allowed = (band_key > band_row) & (band_key <= band_row + WIN)

        def linear_part(request, stream):
            state = states[request]
            state_sums = state[:terms].reshape(terms, heads, HS)
            state_norms = state[terms : terms + 2].reshape(-1)[: terms * heads].reshape(terms, heads)
            tail = state[terms + 2 + 2 * WIN : terms + 2 + 2 * WIN + KC - 1]
            normed = rms_norm(stream, norm_first)
            queries = dot(normed, query_weight).astype(BF).reshape(LMAX, heads, FD)
            key_rows = dot(normed, key_weight).astype(BF).reshape(LMAX, heads, FD)
            values = dot(normed, value_weight).astype(BF)
            gating = dot(normed, filter_gate).astype(BF)
            extended = jnp.concatenate([tail, values], axis=0).astype(F32)
            convolved = sum(
                filter_taps[offset] * extended[KC - 1 - offset : KC - 1 - offset + LMAX]
                for offset in range(KC)
            )
            mixed = (convolved * jax.nn.silu(gating.astype(F32))).astype(BF)
            mixed = mixed.reshape(LMAX, heads, HS)
            scores = jnp.einsum("thf,shf->hts", queries, key_rows, preferred_element_type=F32)
            scores = scores * FD ** (-0.5)
            weights = jnp.where(causal, 1.0 + scores + 0.5 * scores * scores, 0.0)
            mapped = folded_features(queries)
            numerator = jnp.einsum(
                "hts,shd->thd", weights.astype(BF), mixed, preferred_element_type=F32
            ) + jnp.einsum(
                "htf,fhd->thd", mapped.astype(BF), state_sums, preferred_element_type=F32
            )
            denominator = jnp.sum(weights, axis=-1) + jnp.sum(
                mapped * jnp.transpose(state_norms).astype(F32)[:, None, :], axis=-1
            )
            linear_rows = (numerator / jnp.transpose(denominator)[..., None]).astype(BF)
            return dot(linear_rows.reshape(LMAX, width), linear_out).astype(BF)

        def window_part(request, stream):
            state = states[request]
            normed = rms_norm(stream, norm_second)
            queries = dot(normed, window_query).astype(BF).reshape(bands, WIN, heads, HS)
            key_rows = dot(normed, window_key).astype(BF)
            value_rows = dot(normed, window_value).astype(BF)
            start = terms + 2

            def paired(prefix, rows):
                blocks = jnp.concatenate([prefix, rows]).reshape(bands + 1, WIN, heads, HS)
                return jnp.concatenate([blocks[:-1], blocks[1:]], axis=1)

            key_pairs = paired(state[start : start + WIN], key_rows)
            value_pairs = paired(state[start + WIN : start + 2 * WIN], value_rows)
            logits = jnp.einsum(
                "bthd,bphd->bhtp", queries, key_pairs, preferred_element_type=F32
            ) * HS ** (-0.5)
            logits = jnp.where(allowed, logits, -jnp.inf)
            row_max = jnp.max(logits, axis=-1, keepdims=True)
            exponent = jnp.exp(logits - row_max)
            chances = (exponent / jnp.sum(exponent, axis=-1, keepdims=True)).astype(BF)
            attended = jnp.einsum(
                "bhtp,bphd->bthd", chances, value_pairs, preferred_element_type=F32
            ).astype(BF)
            final = (position == suffix_len[request] - 1).reshape(bands, 1, WIN)
            top = jnp.max(jnp.where(final, row_max[..., 0], -jnp.inf))
            return dot(attended.reshape(LMAX, width), window_out).astype(BF), top

        def hidden_part(stream):
            normed = rms_norm(stream, norm_third)
            inner = (jax.nn.silu(dot(normed, gate_weight)) * dot(normed, up_weight)).astype(BF)
            return dot(inner, down_weight).astype(BF)

        here = lax.axis_index("tensor")
        row_start = here * share_rows
        rows_here = row_start + jnp.arange(share_rows)
        outs, squares, tops = [], [], []
        for request in range(requests_here):
            stream = line_gather(hidden[request], "tensor", tensor_count)
            partial = linear_part(request, stream)
            stream = settle(partial, stream, "tensor", tensor_count)
            partial, top = window_part(request, stream)
            stream = settle(partial, stream, "tensor", tensor_count)
            partial = hidden_part(stream)
            total = line_scatter(partial, "tensor", tensor_count)
            mine = lax.dynamic_slice_in_dim(stream, row_start, share_rows, 0).astype(F32)
            mine = (mine + total).astype(BF)
            live = (rows_here < suffix_len[request])[:, None]
            outs.append(jnp.where(live, mine, jnp.zeros_like(mine)))
            floats = mine.astype(F32)
            squares.append(jnp.sum(jnp.where(live, floats * floats, 0.0)))
            tops.append(top)
        scalars = lax.all_gather(jnp.stack(squares + tops), "tensor")
        total = jnp.sum(scalars[:, :requests_here], axis=0)
        top_logit = jnp.max(scalars[:, requests_here:], axis=0)
        return jnp.stack(outs), jnp.sqrt(total / D), top_logit

    return per_device


def solution(mesh):
    return jax.shard_map(
        make(mesh.shape["req"], mesh.shape["tensor"]),
        mesh=mesh,
        in_specs=(
            P("req", "tensor", None),
            P("req"),
            P("req"),
            P(),
            P(),
            P(None, "tensor"),
            P(None, "tensor"),
            P(None, "tensor"),
            P(None, "tensor"),
            P(None, "tensor"),
            P("tensor", None),
            P(),
            P(None, "tensor"),
            P(None, "tensor"),
            P(None, "tensor"),
            P("tensor", None),
            P(),
            P(None, "tensor"),
            P(None, "tensor"),
            P("tensor", None),
            P("req", "tensor", None, None),
            P("req", "tensor", None),
            P("req", None, "tensor"),
            P("req", None, "tensor"),
            P("req", None, "tensor"),
        ),
        out_specs=(P("req", "tensor", None), P("req"), P("req")),
        check_vma=False,
    )
```

time: 728 us -> 718 us (0.986)
  waiting for transfers between devices: 508 us -> 288 us
  local copies, waits for them, and re-layouts: 27.7 us -> 123 us
  starting transfers between devices: 0.7 us -> 88 us
  other arithmetic: 42.6 us -> 71.6 us
  matrix products: 84.7 us -> 107 us
  blocking collectives: 39.4 us -> 23 us
  between operations: 15.1 us -> 5.3 us
    psum x3 -> x0, waiting for transfers between devices: 400 us -> none  [settle(): lax.psum(partial_sum.astype(jnp.bfloat16), 'tensor').astype(jnp.float32)]
    ppermute x0 -> x51, waiting for transfers between devices: none -> 288 us  [the longest x4 58.2 us: middle_exchange(): near_in = lax.ppermute(near, axis, inward)]
    all_gather x4 -> x0, waiting for transfers between devices: 105 us -> none  [the longest x1 50.2 us: per_device(): stream = lax.all_gather(hidden, 'tensor', axis=1, tiled=True)]
    ppermute x0 -> x51, starting transfers between devices: none -> 88 us  [the longest x6 18.3 us: line_scatter(): up = lax.ppermute(to_up, axis, [(i, i + 1) for i in range(step)])]
    slice x1 -> x58, local copies, waits for them, and re-layouts: 0.01 us -> 43.9 us  [the longest x16 37 us: paired(): return jnp.concatenate([blocks[:-1], blocks[1:]], axis=1)]
    concatenate x5, local copies, waits for them, and re-layouts: 3.98 us -> 34.6 us  [the longest x2 33.6 us: folded_features(): return jnp.concatenate(parts, axis=-1)]
    unnamed x0 -> x2, blocking collectives: none -> 23 us
    dot_general x17 -> x34, matrix products: 84.7 us -> 107 us  [the longest x22 79.2 us: dot(): return jnp.dot(left, right, preferred_element_type=F32)]
  transfers between devices with their start and end apart: 7 -> 51, of which waited for: 7 -> 25; matrix products, arithmetic and copies ran while one was open for 9% -> 30% of each run, Pallas kernels for 0% -> 0%
where the time goes in v1:
time: 718 us; the launch traced here: 705 us
  waiting for transfers between devices  288 us (40%)
  local copies, waits for them, and re-layouts  123 us (17%)
  matrix products  107 us (15%)
  starting transfers between devices  88 us (12%)
  other arithmetic  71.6 us (10%)
  blocking collectives  23 us (3%)
    dot_general x22, matrix products, dot(): return jnp.dot(left, right, preferred_element_type=F32)  79.2 us
    ppermute x4, waiting for transfers between devices, middle_exchange(): near_in = lax.ppermute(near, axis, inward)  58.2 us
    ppermute x4, waiting for transfers between devices, middle_exchange(): other_out = lax.ppermute(other, axis, outward)  55.7 us
    ppermute x4, waiting for transfers between devices, middle_exchange(): own_out = lax.ppermute(own, axis, outward)  49.5 us
    slice x16, local copies, waits for them, and re-layouts, paired(): return jnp.concatenate([blocks[:-1], blocks[1:]], axis=1)  37 us
    concatenate x2, local copies, waits for them, and re-layouts, folded_features(): return jnp.concatenate(parts, axis=-1)  33.6 us
    ppermute x6, waiting for transfers between devices, line_gather(): down = lax.ppermute(down, axis, [(i + 1, i) for i in range(count - step)])  33.1 us
    ppermute x4, waiting for transfers between devices, middle_exchange(): far_in = lax.ppermute(far, axis, inward)  30 us
  transfers between devices with their start and end apart: 51, of which 25 were waited for; matrix products, arithmetic and copies ran while one was open for 30% of the time, Pallas kernels for 0%

profile of v1, /device:TPU:0, one launch (start us, length us, event | category | flops | bytes accessed | tf_op | source)
XLA Modules:
  0.0 705.5 jit_solution(15969673366671493209)
XLA Ops:
  2.9 5.9 collective-permute-start
  10.1 5.3 collective-permute-start.27
  19.6 8.0 %all-reduce.2 = s32[16]{0:T(128)S(1)} all-reduce(s32[16]{0:T(128)S(1)} %dynamic-update-slice), channel_id=1, replica_groups=mesh['req'=8,'tensor'=4] {'req'}, use_global_device_ids=true, to_apply=%add.2 | all-reduce | flops 16 | bytes 128
  50.8 14.0 %collective-permute-done.4 = bf16[128,1792]{1,0:T(8,128)(2,1)S(1)} collective-permute-done((bf16[128,1792]{1,0:T(8,128)(2,1)}, bf16[128,1792]{1,0:T(8,128)(2,1)S(1)}, u32[]{:S(2)}, u32[]{:S(2)}) %collective-permute-start.4) | collective-permute-done | bytes 458784 | tf_op jit(solution)/shard_map/ppermute | solution.py:56
  66.1 8.5 %collective-permute-done.31 = bf16[128,1792]{1,0:T(8,128)(2,1)S(1)} collective-permute-done((bf16[128,1792]{1,0:T(8,128)(2,1)}, bf16[128,1792]{1,0:T(8,128)(2,1)S(1)}, u32[]{:S(2)}, u32[]{:S(2)}) %collective-permute-start.31) | collective-permute-done | bytes 458784 | tf_op jit(solution)/shard_map/ppermute | solution.py:56
  84.5 7.6 %collective-permute-done.32 = bf16[128,1792]{1,0:T(8,128)(2,1)S(1)} collective-permute-done((bf16[128,1792]{1,0:T(8,128)(2,1)S(1)}, bf16[128,1792]{1,0:T(8,128)(2,1)S(1)}, u32[]{:S(2)}, u32[]{:S(2)}) %collective-permute-start.32) | collective-permute-done | bytes 458784 | tf_op jit(solution)/shard_map/ppermute | solution.py:56
  98.4 16.9 %concatenate.149 = f32[4,512,161]{1,2,0:T(8,128)} concatenate(f32[4,512,1]{1,2,0:T(1,128)S(1)} %broadcast.605, f32[4,512,16]{1,2,0:T(8,128)S(1)} %get-tuple-element.66, f32[4,512,16]{1,2,0:T(8,128)S(1)} %get-tuple-element.67, f32[4,512,16]{1,2,0:T(8,128)S(1)} %get-tuple-element.68, f32[4,512,16]{1,2,0:T(8,128)S(1)} %get-tuple-element.69, f32[4,512,16]{1,2,0:T(8,128)S(1)} %get-tuple-element.70, ...), dimensions={2} | concatenate | bytes 2637824 | tf_op jit(solution)/shard_map/concatenate | solution.py:34
  116.5 16.7 %concatenate.132 = f32[4,512,161]{1,2,0:T(8,128)} concatenate(f32[4,512,1]{1,2,0:T(1,128)S(1)} %broadcast.605, f32[4,512,16]{1,2,0:T(8,128)S(1)} %get-tuple-element.56, f32[4,512,16]{1,2,0:T(8,128)S(1)} %get-tuple-element.57, f32[4,512,16]{1,2,0:T(8,128)S(1)} %get-tuple-element.58, f32[4,512,16]{1,2,0:T(8,128)S(1)} %get-tuple-element.59, f32[4,512,16]{1,2,0:T(8,128)S(1)} %get-tuple-element.60, ...), dimensions={2} | concatenate | bytes 2637824 | tf_op jit(solution)/shard_map/concatenate | solution.py:34
  158.9 14.5 %collective-permute-done.7 = bf16[2,2,160,896]{3,2,1,0:T(8,128)(2,1)} collective-permute-done((bf16[2,2,160,896]{3,2,1,0:T(8,128)(2,1)S(1)}, bf16[2,2,160,896]{3,2,1,0:T(8,128)(2,1)}, u32[]{:S(2)}, u32[]{:S(2)}) %collective-permute-start.7) | collective-permute-done | bytes 1146912 | tf_op jit(solution)/shard_map/ppermute | solution.py:124
  180.1 5.9 fusion.18
  186.0 5.4 collective-permute-done.8
  223.6 5.7 collective-permute-done.34
  238.2 10.6 %collective-permute-done.10 = bf16[256,1792]{1,0:T(8,128)(2,1)} collective-permute-done((bf16[256,1792]{1,0:T(8,128)(2,1)S(1)}, bf16[256,1792]{1,0:T(8,128)(2,1)}, u32[]{:S(2)}, u32[]{:S(2)}) %collective-permute-start.10) | collective-permute-done | bytes 917536 | tf_op jit(solution)/shard_map/ppermute | solution.py:93
  251.1 17.4 %collective-permute-done.33 = bf16[256,1792]{1,0:T(8,128)(2,1)} collective-permute-done((bf16[256,1792]{1,0:T(8,128)(2,1)S(1)}, bf16[256,1792]{1,0:T(8,128)(2,1)}, u32[]{:S(2)}, u32[]{:S(2)}) %collective-permute-start.33) | collective-permute-done | bytes 917536 | tf_op jit(solution)/shard_map/ppermute | solution.py:94
  272.0 11.4 %collective-permute-done.9 = bf16[256,1792]{1,0:T(8,128)(2,1)S(1)} collective-permute-done((bf16[256,1792]{1,0:T(8,128)(2,1)}, bf16[256,1792]{1,0:T(8,128)(2,1)S(1)}, u32[]{:S(2)}, u32[]{:S(2)}) %collective-permute-start.9) | collective-permute-done | bytes 917536 | tf_op jit(solution)/shard_map/ppermute | solution.py:94
  293.4 19.7 %collective-permute-done.36 = bf16[256,1792]{1,0:T(8,128)(2,1)} collective-permute-done((bf16[256,1792]{1,0:T(8,128)(2,1)S(1)}, bf16[256,1792]{1,0:T(8,128)(2,1)}, u32[]{:S(2)}, u32[]{:S(2)}) %collective-permute-start.36) | collective-permute-done | bytes 917536 | tf_op jit(solution)/shard_map/ppermute | solution.py:99
  313.1 19.7 %collective-permute-done.38 = bf16[256,1792]{1,0:T(8,128)(2,1)} collective-permute-done((bf16[256,1792]{1,0:T(8,128)(2,1)S(1)}, bf16[256,1792]{1,0:T(8,128)(2,1)}, u32[]{:S(2)}, u32[]{:S(2)}) %collective-permute-start.38) | collective-permute-done | bytes 917536 | tf_op jit(solution)/shard_map/ppermute | solution.py:100
  338.7 13.6 %collective-permute-done.12 = bf16[256,1792]{1,0:T(8,128)(2,1)S(1)} collective-permute-done((bf16[256,1792]{1,0:T(8,128)(2,1)}, bf16[256,1792]{1,0:T(8,128)(2,1)S(1)}, u32[]{:S(2)}, u32[]{:S(2)}) %collective-permute-start.12) | collective-permute-done | bytes 917536 | tf_op jit(solution)/shard_map/ppermute | solution.py:99
  352.3 14.2 %collective-permute-done.14 = bf16[256,1792]{1,0:T(8,128)(2,1)S(1)} collective-permute-done((bf16[256,1792]{1,0:T(8,128)(2,1)}, bf16[256,1792]{1,0:T(8,128)(2,1)S(1)}, u32[]{:S(2)}, u32[]{:S(2)}) %collective-permute-start.14) | collective-permute-done | bytes 917536 | tf_op jit(solution)/shard_map/ppermute | solution.py:100
  460.5 13.7 %collective-permute-done.16 = bf16[256,1792]{1,0:T(8,128)(2,1)S(1)} collective-permute-done((bf16[256,1792]{1,0:T(8,128)(2,1)S(1)}, bf16[256,1792]{1,0:T(8,128)(2,1)S(1)}, u32[]{:S(2)}, u32[]{:S(2)}) %collective-permute-start.16) | collective-permute-done | bytes 917536 | tf_op jit(solution)/shard_map/ppermute | solution.py:93
  475.3 18.6 %collective-permute-done.39 = bf16[256,1792]{1,0:T(8,128)(2,1)S(1)} collective-permute-done((bf16[256,1792]{1,0:T(8,128)(2,1)S(1)}, bf16[256,1792]{1,0:T(8,128)(2,1)S(1)}, u32[]{:S(2)}, u32[]{:S(2)}) %collective-permute-start.39) | collective-permute-done | bytes 917536 | tf_op jit(solution)/shard_map/ppermute | solution.py:94
  496.3 10.8 %collective-permute-done.15 = bf16[256,1792]{1,0:T(8,128)(2,1)S(1)} collective-permute-done((bf16[256,1792]{1,0:T(8,128)(2,1)S(1)}, bf16[256,1792]{1,0:T(8,128)(2,1)S(1)}, u32[]{:S(2)}, u32[]{:S(2)}) %collective-permute-start.15) | collective-permute-done | bytes 917536 | tf_op jit(solution)/shard_map/ppermute | solution.py:94
  521.0 16.2 %collective-permute-done.42 = bf16[256,1792]{1,0:T(8,128)(2,1)S(1)} collective-permute-done((bf16[256,1792]{1,0:T(8,128)(2,1)}, bf16[256,1792]{1,0:T(8,128)(2,1)S(1)}, u32[]{:S(2)}, u32[]{:S(2)}) %collective-permute-start.42) | collective-permute-done | bytes 917536 | tf_op jit(solution)/shard_map/ppermute | solution.py:99
  538.2 18.8 %collective-permute-done.44 = bf16[256,1792]{1,0:T(8,128)(2,1)} collective-permute-done((bf16[256,1792]{1,0:T(8,128)(2,1)S(1)}, bf16[256,1792]{1,0:T(8,128)(2,1)}, u32[]{:S(2)}, u32[]{:S(2)}) %collective-permute-start.44) | collective-permute-done | bytes 917536 | tf_op jit(solution)/shard_map/ppermute | solution.py:100
  559.1 8.2 %fusion.145 = f32[512,1792]{1,0:T(8,128)} fusion(bf16[1792,1792]{1,0:T(8,128)(2,1)} %param.42, f32[512]{0:T(512)S(1)} %add_rsqrt_fusion, f32[1792]{0:T(1024)S(1)} %copy-done.67, bf16[256,1792]{1,0:T(8,128)(2,1)S(1)} %get-tuple-element.18, bf16[256,1792]{1,0:T(8,128)(2,1)S(1)} %get-tuple-element.17), kind=kOutput, calls=%fused_computation.362 | convolution fusion | flops 3294756864 | bytes 11936768 | tf_op jit(solution)/shard_map/dot_general | solution.py:26
  567.3 14.2 %convolution_convert_fusion = bf16[512,1792]{1,0:T(8,128)(2,1)} fusion(bf16[1792,1792]{1,0:T(8,128)(2,1)} %param.44, f32[512,1792]{1,0:T(8,128)} %fusion.145, bf16[1792,1792]{1,0:T(8,128)(2,1)} %param.43, f32[512]{0:T(512)S(1)} %add_rsqrt_fusion, f32[1792]{0:T(1024)S(1)} %copy-done.67, bf16[256,1792]{1,0:T(8,128)(2,1)S(1)} %get-tuple-element.18, ...), kind=kOutput, calls=%fused_computation.37 | convolution fusion | flops 6589513728 | bytes 20194304 | tf_op jit(solution)/shard_map/dot_general | solution.py:26
  591.3 8.2 %fusion.149 = f32[512,1792]{1,0:T(8,128)} fusion(bf16[1792,1792]{1,0:T(8,128)(2,1)} %param.42, f32[1792]{0:T(1024)S(1)} %copy-done.67, f32[512]{0:T(512)S(1)} %add_rsqrt_fusion.3, bf16[256,1792]{1,0:T(8,128)(2,1)S(1)} %get-tuple-element.14, bf16[256,1792]{1,0:T(8,128)(2,1)S(1)} %get-tuple-element.13), kind=kOutput, calls=%fused_computation.363 | convolution fusion | flops 3294756864 | bytes 11936768 | tf_op jit(solution)/shard_map/dot_general | solution.py:26
  599.5 14.4 %convolution_convert_fusion.3 = bf16[512,1792]{1,0:T(8,128)(2,1)} fusion(bf16[1792,1792]{1,0:T(8,128)(2,1)} %param.44, f32[512,1792]{1,0:T(8,128)} %fusion.149, bf16[1792,1792]{1,0:T(8,128)(2,1)} %param.43, f32[1792]{0:T(1024)S(1)} %copy-done.67, f32[512]{0:T(512)S(1)} %add_rsqrt_fusion.3, bf16[256,1792]{1,0:T(8,128)(2,1)} %copy-done.5, ...), kind=kOutput, calls=%fused_computation.40 | convolution fusion | flops 6589513728 | bytes 20194304 | tf_op jit(solution)/shard_map/dot_general | solution.py:26
  619.3 8.3 %collective-permute-done.21 = bf16[128,1792]{1,0:T(8,128)(2,1)S(1)} collective-permute-done((bf16[128,1792]{1,0:T(8,128)(2,1)S(1)}, bf16[128,1792]{1,0:T(8,128)(2,1)S(1)}, u32[]{:S(2)}, u32[]{:S(2)}) %collective-permute-start.21) | collective-permute-done | bytes 458784 | tf_op jit(solution)/shard_map/ppermute | solution.py:76
  657.2 16.3 %collective-permute-done.50 = bf16[128,1792]{1,0:T(8,128)(2,1)S(1)} collective-permute-done((bf16[128,1792]{1,0:T(8,128)(2,1)S(1)}, bf16[128,1792]{1,0:T(8,128)(2,1)S(1)}, u32[]{:S(2)}, u32[]{:S(2)}) %collective-permute-start.50) | collective-permute-done | bytes 458784 | tf_op jit(solution)/shard_map/ppermute | solution.py:77
  675.5 7.6 %collective-permute-done.26 = bf16[128,1792]{1,0:T(8,128)(2,1)S(1)} collective-permute-done((bf16[128,1792]{1,0:T(8,128)(2,1)S(1)}, bf16[128,1792]{1,0:T(8,128)(2,1)S(1)}, u32[]{:S(2)}, u32[]{:S(2)}) %collective-permute-start.26) | collective-permute-done | bytes 458784 | tf_op jit(solution)/shard_map/ppermute | solution.py:77
  687.0 15.0 %all-reduce.3 = f32[16]{0:T(128)S(1)} all-reduce(f32[16]{0:T(128)S(1)} %maximum_dynamic-update-slice_fusion), channel_id=2, replica_groups=mesh['req'=8,'tensor'=4] {'tensor'}, use_global_device_ids=true, to_apply=%add.3 | all-reduce | flops 16 | bytes 128
  (439 shorter events, 308.8 us)
Async XLA Ops:
  2.9 35.5 %collective-permute-start = (bf16[128,1792]{1,0:T(8,128)(2,1)}, bf16[128,1792]{1,0:T(8,128)(2,1)}, u32[]{:S(2)}, u32[]{:S(2)}) collective-permute-start(bf16[128,1792]{1,0:T(8,128)(2,1)} %get-tuple-element.47), channel_id=1, source_target_pairs={{0,1},{1,2},{2,3},{4,5},{5,6},{6,7},{8,9},{9,10},{10,11},{12,13},{... | collective-permute-start | bytes 1376264 | tf_op jit(solution)/shard_map/ppermute | solution.py:55
  8.8 34.2 %collective-permute-start.3 = (bf16[128,1792]{1,0:T(8,128)(2,1)}, bf16[128,1792]{1,0:T(8,128)(2,1)}, u32[]{:S(2)}, u32[]{:S(2)}) collective-permute-start(bf16[128,1792]{1,0:T(8,128)(2,1)} %get-tuple-element.47), channel_id=1, source_target_pairs={{1,0},{2,1},{3,2},{5,4},{6,5},{7,6},{9,8},{10,9},{11,10},{13,12},{... | collective-permute-start | bytes 1376264 | tf_op jit(solution)/shard_map/ppermute | solution.py:56
  10.1 32.1 %collective-permute-start.27 = (bf16[128,1792]{1,0:T(8,128)(2,1)}, bf16[128,1792]{1,0:T(8,128)(2,1)}, u32[]{:S(2)}, u32[]{:S(2)}) collective-permute-start(bf16[128,1792]{1,0:T(8,128)(2,1)} %get-tuple-element.48), channel_id=1, source_target_pairs={{0,1},{1,2},{2,3},{4,5},{5,6},{6,7},{8,9},{9,10},{10,11},{12,13},{... | collective-permute-start | bytes 1376264 | tf_op jit(solution)/shard_map/ppermute | solution.py:55
  15.4 28.9 %collective-permute-start.30 = (bf16[128,1792]{1,0:T(8,128)(2,1)}, bf16[128,1792]{1,0:T(8,128)(2,1)}, u32[]{:S(2)}, u32[]{:S(2)}) collective-permute-start(bf16[128,1792]{1,0:T(8,128)(2,1)} %get-tuple-element.48), channel_id=1, source_target_pairs={{1,0},{2,1},{3,2},{5,4},{6,5},{7,6},{9,8},{10,9},{11,10},{13,12},{... | collective-permute-start | bytes 1376264 | tf_op jit(solution)/shard_map/ppermute | solution.py:56
  44.3 30.3 %collective-permute-start.31 = (bf16[128,1792]{1,0:T(8,128)(2,1)}, bf16[128,1792]{1,0:T(8,128)(2,1)S(1)}, u32[]{:S(2)}, u32[]{:S(2)}) collective-permute-start(bf16[128,1792]{1,0:T(8,128)(2,1)} %collective-permute-done.30), channel_id=1, source_target_pairs={{1,0},{2,1},{5,4},{6,5},{9,8},{10,9},{13,12},{14,13},{17,16},{18,1... | collective-permute-start | bytes 1376264 | tf_op jit(solution)/shard_map/ppermute | solution.py:56
  45.6 30.3 %collective-permute-start.2 = (bf16[128,1792]{1,0:T(8,128)(2,1)S(1)}, bf16[128,1792]{1,0:T(8,128)(2,1)}, u32[]{:S(2)}, u32[]{:S(2)}) collective-permute-start(bf16[128,1792]{1,0:T(8,128)(2,1)S(1)} %collective-permute-done.1), channel_id=1, source_target_pairs={{2,3},{6,7},{10,11},{14,15},{18,19},{22,23},{26,27},{30,31}} | collective-permute-start | bytes 1376264 | tf_op jit(solution)/shard_map/ppermute | solution.py:55
  48.7 86.7 %collective-permute-start.6 = (bf16[4,2,160,896]{3,2,1,0:T(8,128)(2,1)}, bf16[4,2,160,896]{3,2,1,0:T(8,128)(2,1)}, u32[]{:S(2)}, u32[]{:S(2)}) collective-permute-start(bf16[4,2,160,896]{3,2,1,0:T(8,128)(2,1)} %fusion.22), channel_id=1, source_target_pairs={{0,4},{4,0},{8,12},{12,8},{16,20},{20,16},{24,28},{28,24},{1,5},{5... | collective-permute-start | bytes 6881288 | tf_op jit(solution)/shard_map/ppermute | solution.py:124
  50.1 28.0 %collective-permute-start.29 = (bf16[128,1792]{1,0:T(8,128)(2,1)S(1)}, bf16[128,1792]{1,0:T(8,128)(2,1)S(1)}, u32[]{:S(2)}, u32[]{:S(2)}) collective-permute-start(bf16[128,1792]{1,0:T(8,128)(2,1)S(1)} %collective-permute-done.28), channel_id=1, source_target_pairs={{2,3},{6,7},{10,11},{14,15},{18,19},{22,23},{26,27},{30,31}} | collective-permute-start | bytes 1376264 | tf_op jit(solution)/shard_map/ppermute | solution.py:55
  148.2 25.2 %collective-permute-start.7 = (bf16[2,2,160,896]{3,2,1,0:T(8,128)(2,1)S(1)}, bf16[2,2,160,896]{3,2,1,0:T(8,128)(2,1)}, u32[]{:S(2)}, u32[]{:S(2)}) collective-permute-start(bf16[2,2,160,896]{3,2,1,0:T(8,128)(2,1)S(1)} %copy.139), channel_id=1, source_target_pairs={{0,8},{4,12},{8,0},{12,4},{16,24},{20,28},{24,16},{28,20},{1,9},{5... | collective-permute-start | bytes 3440648 | tf_op jit(solution)/shard_map/ppermute | solution.py:124
  206.5 22.8 %collective-permute-start.34 = (bf16[256,1792]{1,0:T(8,128)(2,1)}, bf16[256,1792]{1,0:T(8,128)(2,1)}, u32[]{:S(2)}, u32[]{:S(2)}) collective-permute-start(bf16[256,1792]{1,0:T(8,128)(2,1)} %get-tuple-element.34), channel_id=1, source_target_pairs={{0,1},{3,2},{4,5},{7,6},{8,9},{11,10},{12,13},{15,14},{16,17},{19,... | collective-permute-start | bytes 2752520 | tf_op jit(solution)/shard_map/ppermute | solution.py:93
  219.1 29.7 %collective-permute-start.10 = (bf16[256,1792]{1,0:T(8,128)(2,1)S(1)}, bf16[256,1792]{1,0:T(8,128)(2,1)}, u32[]{:S(2)}, u32[]{:S(2)}) collective-permute-start(bf16[256,1792]{1,0:T(8,128)(2,1)S(1)} %get-tuple-element.28), channel_id=1, source_target_pairs={{0,1},{3,2},{4,5},{7,6},{8,9},{11,10},{12,13},{15,14},{16,17},{19,... | collective-permute-start | bytes 2752520 | tf_op jit(solution)/shard_map/ppermute | solution.py:93
  221.4 47.1 %collective-permute-start.33 = (bf16[256,1792]{1,0:T(8,128)(2,1)S(1)}, bf16[256,1792]{1,0:T(8,128)(2,1)}, u32[]{:S(2)}, u32[]{:S(2)}) collective-permute-start(bf16[256,1792]{1,0:T(8,128)(2,1)S(1)} %copy-done.22), channel_id=1, source_target_pairs={{0,1},{3,2},{4,5},{7,6},{8,9},{11,10},{12,13},{15,14},{16,17},{19,... | collective-permute-start | bytes 2752520 | tf_op jit(solution)/shard_map/ppermute | solution.py:94
  231.9 36.6 %collective-permute-start.35 = (bf16[256,1792]{1,0:T(8,128)(2,1)}, bf16[256,1792]{1,0:T(8,128)(2,1)}, u32[]{:S(2)}, u32[]{:S(2)}) collective-permute-start(bf16[256,1792]{1,0:T(8,128)(2,1)} %add.505), channel_id=1, source_target_pairs={{1,2},{2,1},{5,6},{6,5},{9,10},{10,9},{13,14},{14,13},{17,18},{18,... | collective-permute-start | bytes 2752520 | tf_op jit(solution)/shard_map/ppermute | solution.py:95
  233.5 49.9 %collective-permute-start.9 = (bf16[256,1792]{1,0:T(8,128)(2,1)}, bf16[256,1792]{1,0:T(8,128)(2,1)S(1)}, u32[]{:S(2)}, u32[]{:S(2)}) collective-permute-start(bf16[256,1792]{1,0:T(8,128)(2,1)} %get-tuple-element.27), channel_id=1, source_target_pairs={{0,1},{3,2},{4,5},{7,6},{8,9},{11,10},{12,13},{15,14},{16,17},{19,... | collective-permute-start | bytes 2752520 | tf_op jit(solution)/shard_map/ppermute | solution.py:94
  250.2 33.2 %collective-permute-start.11 = (bf16[256,1792]{1,0:T(8,128)(2,1)S(1)}, bf16[256,1792]{1,0:T(8,128)(2,1)S(1)}, u32[]{:S(2)}, u32[]{:S(2)}) collective-permute-start(bf16[256,1792]{1,0:T(8,128)(2,1)S(1)} %add.465), channel_id=1, source_target_pairs={{1,2},{2,1},{5,6},{6,5},{9,10},{10,9},{13,14},{14,13},{17,18},{18,... | collective-permute-start | bytes 2752520 | tf_op jit(solution)/shard_map/ppermute | solution.py:95
  287.8 25.4 %collective-permute-start.36 = (bf16[256,1792]{1,0:T(8,128)(2,1)S(1)}, bf16[256,1792]{1,0:T(8,128)(2,1)}, u32[]{:S(2)}, u32[]{:S(2)}) collective-permute-start(bf16[256,1792]{1,0:T(8,128)(2,1)S(1)} %add_convert_fusion.1), channel_id=1, source_target_pairs={{1,0},{2,3},{5,4},{6,7},{9,8},{10,11},{13,12},{14,15},{17,16},{18,... | collective-permute-start | bytes 2752520 | tf_op jit(solution)/shard_map/ppermute | solution.py:99
  289.1 43.7 %collective-permute-start.38 = (bf16[256,1792]{1,0:T(8,128)(2,1)S(1)}, bf16[256,1792]{1,0:T(8,128)(2,1)}, u32[]{:S(2)}, u32[]{:S(2)}) collective-permute-start(bf16[256,1792]{1,0:T(8,128)(2,1)S(1)} %collective-permute-done.37), channel_id=1, source_target_pairs={{1,0},{2,3},{5,4},{6,7},{9,8},{10,11},{13,12},{14,15},{17,16},{18,... | collective-permute-start | bytes 2752520 | tf_op jit(solution)/shard_map/ppermute | solution.py:100
  290.7 61.6 %collective-permute-start.12 = (bf16[256,1792]{1,0:T(8,128)(2,1)}, bf16[256,1792]{1,0:T(8,128)(2,1)S(1)}, u32[]{:S(2)}, u32[]{:S(2)}) collective-permute-start(bf16[256,1792]{1,0:T(8,128)(2,1)} %add_convert_fusion.3), channel_id=1, source_target_pairs={{1,0},{2,3},{5,4},{6,7},{9,8},{10,11},{13,12},{14,15},{17,16},{18,... | collective-permute-start | bytes 2752520 | tf_op jit(solution)/shard_map/ppermute | solution.py:99
  292.1 74.4 %collective-permute-start.14 = (bf16[256,1792]{1,0:T(8,128)(2,1)}, bf16[256,1792]{1,0:T(8,128)(2,1)S(1)}, u32[]{:S(2)}, u32[]{:S(2)}) collective-permute-start(bf16[256,1792]{1,0:T(8,128)(2,1)} %collective-permute-done.13), channel_id=1, source_target_pairs={{1,0},{2,3},{5,4},{6,7},{9,8},{10,11},{13,12},{14,15},{17,16},{18,... | collective-permute-start | bytes 2752520 | tf_op jit(solution)/shard_map/ppermute | solution.py:100
  411.9 42.9 %collective-permute-start.40 = (bf16[256,1792]{1,0:T(8,128)(2,1)}, bf16[256,1792]{1,0:T(8,128)(2,1)}, u32[]{:S(2)}, u32[]{:S(2)}) collective-permute-start(bf16[256,1792]{1,0:T(8,128)(2,1)} %get-tuple-element.32), channel_id=1, source_target_pairs={{0,1},{3,2},{4,5},{7,6},{8,9},{11,10},{12,13},{15,14},{16,17},{19,... | collective-permute-start | bytes 2752520 | tf_op jit(solution)/shard_map/ppermute | solution.py:93
  452.0 22.2 %collective-permute-start.16 = (bf16[256,1792]{1,0:T(8,128)(2,1)S(1)}, bf16[256,1792]{1,0:T(8,128)(2,1)S(1)}, u32[]{:S(2)}, u32[]{:S(2)}) collective-permute-start(bf16[256,1792]{1,0:T(8,128)(2,1)S(1)} %get-tuple-element.26), channel_id=1, source_target_pairs={{0,1},{3,2},{4,5},{7,6},{8,9},{11,10},{12,13},{15,14},{16,17},{19,... | collective-permute-start | bytes 2752520 | tf_op jit(solution)/shard_map/ppermute | solution.py:93
  453.5 40.4 %collective-permute-start.39 = (bf16[256,1792]{1,0:T(8,128)(2,1)S(1)}, bf16[256,1792]{1,0:T(8,128)(2,1)S(1)}, u32[]{:S(2)}, u32[]{:S(2)}) collective-permute-start(bf16[256,1792]{1,0:T(8,128)(2,1)S(1)} %copy-done.24), channel_id=1, source_target_pairs={{0,1},{3,2},{4,5},{7,6},{8,9},{11,10},{12,13},{15,14},{16,17},{19,... | collective-permute-start | bytes 2752520 | tf_op jit(solution)/shard_map/ppermute | solution.py:94
  456.5 37.4 %collective-permute-start.41 = (bf16[256,1792]{1,0:T(8,128)(2,1)S(1)}, bf16[256,1792]{1,0:T(8,128)(2,1)S(1)}, u32[]{:S(2)}, u32[]{:S(2)}) collective-permute-start(bf16[256,1792]{1,0:T(8,128)(2,1)S(1)} %add.510), channel_id=1, source_target_pairs={{1,2},{2,1},{5,6},{6,5},{9,10},{10,9},{13,14},{14,13},{17,18},{18,... | collective-permute-start | bytes 2752520 | tf_op jit(solution)/shard_map/ppermute | solution.py:95
  457.2 49.9 %collective-permute-start.15 = (bf16[256,1792]{1,0:T(8,128)(2,1)S(1)}, bf16[256,1792]{1,0:T(8,128)(2,1)S(1)}, u32[]{:S(2)}, u32[]{:S(2)}) collective-permute-start(bf16[256,1792]{1,0:T(8,128)(2,1)S(1)} %get-tuple-element.25), channel_id=1, source_target_pairs={{0,1},{3,2},{4,5},{7,6},{8,9},{11,10},{12,13},{15,14},{16,17},{19,... | collective-permute-start | bytes 2752520 | tf_op jit(solution)/shard_map/ppermute | solution.py:94
  474.4 32.7 %collective-permute-start.17 = (bf16[256,1792]{1,0:T(8,128)(2,1)S(1)}, bf16[256,1792]{1,0:T(8,128)(2,1)S(1)}, u32[]{:S(2)}, u32[]{:S(2)}) collective-permute-start(bf16[256,1792]{1,0:T(8,128)(2,1)S(1)} %add.472), channel_id=1, source_target_pairs={{1,2},{2,1},{5,6},{6,5},{9,10},{10,9},{13,14},{14,13},{17,18},{18,... | collective-permute-start | bytes 2752520 | tf_op jit(solution)/shard_map/ppermute | solution.py:95
  509.3 27.9 %collective-permute-start.42 = (bf16[256,1792]{1,0:T(8,128)(2,1)}, bf16[256,1792]{1,0:T(8,128)(2,1)S(1)}, u32[]{:S(2)}, u32[]{:S(2)}) collective-permute-start(bf16[256,1792]{1,0:T(8,128)(2,1)} %add_convert_fusion), channel_id=1, source_target_pairs={{1,0},{2,3},{5,4},{6,7},{9,8},{10,11},{13,12},{14,15},{17,16},{18,... | collective-permute-start | bytes 2752520 | tf_op jit(solution)/shard_map/ppermute | solution.py:99
  510.7 46.3 %collective-permute-start.44 = (bf16[256,1792]{1,0:T(8,128)(2,1)S(1)}, bf16[256,1792]{1,0:T(8,128)(2,1)}, u32[]{:S(2)}, u32[]{:S(2)}) collective-permute-start(bf16[256,1792]{1,0:T(8,128)(2,1)S(1)} %collective-permute-done.43), channel_id=1, source_target_pairs={{1,0},{2,3},{5,4},{6,7},{9,8},{10,11},{13,12},{14,15},{17,16},{18,... | collective-permute-start | bytes 2752520 | tf_op jit(solution)/shard_map/ppermute | solution.py:100
  517.8 67.8 %collective-permute-start.18 = (bf16[256,1792]{1,0:T(8,128)(2,1)}, bf16[256,1792]{1,0:T(8,128)(2,1)}, u32[]{:S(2)}, u32[]{:S(2)}) collective-permute-start(bf16[256,1792]{1,0:T(8,128)(2,1)} %add_convert_fusion.2), channel_id=1, source_target_pairs={{1,0},{2,3},{5,4},{6,7},{9,8},{10,11},{13,12},{14,15},{17,16},{18,... | collective-permute-start | bytes 2752520 | tf_op jit(solution)/shard_map/ppermute | solution.py:99
  519.2 69.5 %collective-permute-start.20 = (bf16[256,1792]{1,0:T(8,128)(2,1)S(1)}, bf16[256,1792]{1,0:T(8,128)(2,1)}, u32[]{:S(2)}, u32[]{:S(2)}) collective-permute-start(bf16[256,1792]{1,0:T(8,128)(2,1)S(1)} %collective-permute-done.19), channel_id=1, source_target_pairs={{1,0},{2,3},{5,4},{6,7},{9,8},{10,11},{13,12},{14,15},{17,16},{18,... | collective-permute-start | bytes 2752520 | tf_op jit(solution)/shard_map/ppermute | solution.py:100
  583.3 33.3 %collective-permute-start.45 = (bf16[128,1792]{1,0:T(8,128)(2,1)}, bf16[128,1792]{1,0:T(8,128)(2,1)}, u32[]{:S(2)}, u32[]{:S(2)}) collective-permute-start(bf16[128,1792]{1,0:T(8,128)(2,1)} %constant_dynamic-slice_fusion.1), channel_id=1, source_target_pairs={{0,1},{4,5},{8,9},{12,13},{16,17},{20,21},{24,25},{28,29}} | collective-permute-start | bytes 1376264 | tf_op jit(solution)/shard_map/ppermute | solution.py:76
  648.1 27.4 %collective-permute-start.23 = (bf16[128,1792]{1,0:T(8,128)(2,1)S(1)}, bf16[128,1792]{1,0:T(8,128)(2,1)S(1)}, u32[]{:S(2)}, u32[]{:S(2)}) collective-permute-start(bf16[128,1792]{1,0:T(8,128)(2,1)S(1)} %get-tuple-element.23), channel_id=1, source_target_pairs={{0,1},{1,2},{2,3},{4,5},{5,6},{6,7},{8,9},{9,10},{10,11},{12,13},{... | collective-permute-start | bytes 1376264 | tf_op jit(solution)/shard_map/ppermute | solution.py:76
  655.9 27.2 %collective-permute-start.26 = (bf16[128,1792]{1,0:T(8,128)(2,1)S(1)}, bf16[128,1792]{1,0:T(8,128)(2,1)S(1)}, u32[]{:S(2)}, u32[]{:S(2)}) collective-permute-start(bf16[128,1792]{1,0:T(8,128)(2,1)S(1)} %dynamic-slice_add_fusion.5), channel_id=1, source_target_pairs={{1,0},{2,1},{3,2},{5,4},{6,5},{7,6},{9,8},{10,9},{11,10},{13,12},{... | collective-permute-start | bytes 1376264 | tf_op jit(solution)/shard_map/ppermute | solution.py:77
  (88 other events, 1013.8 us)

commit v2 on v1

--- a/solution.py
+++ b/solution.py
@@ -1,6 +1,11 @@
+import functools
+
 import jax
 import jax.numpy as jnp
+import numpy as np
 from jax import lax
+from jax.experimental import pallas as pl
+from jax.experimental.pallas import tpu as pltpu
 from jax.sharding import PartitionSpec as P
 
 D = 1792
@@ -10,10 +15,20 @@
 KC = 3
 LMAX = 512
 PAIRS = FD // 2 + 1
+SQUARES = PAIRS * FD
+FEATURES = 256
+HEAD = 128
+STATE_KEYS = 176
+STATE_VALUES = STATE_KEYS + WIN
+STATE_ROWS = STATE_VALUES + WIN
 
 EPS = 1e-05
 BF = jnp.bfloat16
 F32 = jnp.float32
+MIB = 1 << 20
+ANY = pl.BlockSpec(memory_space=pl.ANY)
+SMEM = pl.BlockSpec(memory_space=pltpu.SMEM)
+VMEM = pl.BlockSpec(memory_space=pltpu.VMEM)
 
 
 def rms_norm(rows, gain):
@@ -24,6 +39,604 @@
 
 def dot(left, right):
     return jnp.dot(left, right, preferred_element_type=F32)
+
+
+def dot_t(left, right):
+    return lax.dot_general(left, right, (((1,), (1,)), ((), ())), preferred_element_type=F32)
+
+
+def fold_matrix():
+    fold = np.zeros((SQUARES + FD + 1, 1 + FD + FD * FD), np.float32)
+    for shift in range(PAIRS):
+        for i in range(FD):
+            j = (i + shift) % FD
+            fold[shift * FD + i, 1 + FD + i * FD + j] = 1.0
+            if 0 < shift < FD // 2:
+                fold[shift * FD + i, 1 + FD + j * FD + i] = 1.0
+    for i in range(FD):
+        fold[SQUARES + i, 1 + i] = 1.0
+    fold[SQUARES + FD, 0] = 1.0
+    return fold
+
+
+def feature_maps(heads):
+    left = np.zeros((heads, HEAD, FEATURES), np.float32)
+    right = np.zeros((heads, HEAD, FEATURES), np.float32)
+    plus = np.zeros((8, FEATURES), np.float32)
+    for head in range(heads):
+        for i in range(FD):
+            for shift in range(PAIRS):
+                left[head, head * FD + i, shift * FD + i] = 1.0
+                right[head, head * FD + (i + shift) % FD, shift * FD + i] = 1.0
+            left[head, head * FD + i, SQUARES + i] = 1.0
+    plus[1, SQUARES : SQUARES + FD] = 1.0
+    plus[0:2, SQUARES + FD] = 1.0
+    plus[2, :SQUARES] = (2.0 * FD) ** (-0.5)
+    plus[2, SQUARES : SQUARES + FD] = FD ** (-0.25)
+    plus[2, SQUARES + FD] = 1.0
+    return left, right, plus
+
+
+def copies(plan, sems):
+    made = []
+    for number, (condition, source, target) in enumerate(plan):
+        copy = pltpu.make_async_copy(source, target, sems.at[number])
+        pl.when(condition)(copy.start)
+        made.append((condition, copy))
+
+    def wait():
+        for condition, copy in made:
+            pl.when(condition)(copy.wait)
+
+    return wait
+
+
+def half_pieces(segments):
+    pieces = ([], [])
+    buffer_row = 0
+    for start, rows in segments:
+        for half in range(2):
+            pieces[half].append((start + half * rows // 2, rows // 2, buffer_row))
+        buffer_row += rows // 2
+    return pieces, buffer_row
+
+
+def put_halves(segments, info, source, near, far, sems):
+    pieces, _ = half_pieces(segments)
+    plan = []
+    for half in range(2):
+        for natural, rows, at in pieces[half]:
+            for low in (0, 1):
+                target = near if half == 1 - low else far
+                plan.append((info[1] == low, source.at[pl.ds(natural, rows)], target.at[pl.ds(at, rows)]))
+    copies(plan, sems)()
+
+
+def halves_plan(segments, info, own, own_out, other, other_out, target):
+    pieces, _ = half_pieces(segments)
+    plan = []
+    for low in (0, 1):
+        for middle in (0, 1):
+            near, far = (own, other) if middle else (own_out, other_out)
+            for half in range(2):
+                source = near if half == 1 - low else far
+                for natural, rows, at in pieces[half]:
+                    plan.append(
+                        (
+                            (info[1] == low) & (info[2] == middle),
+                            source.at[pl.ds(at, rows)],
+                            target.at[pl.ds(natural, rows)],
+                        )
+                    )
+    return plan
+
+
+def lane_of_ones(shape):
+    return (lax.broadcasted_iota(jnp.int32, shape, 1) & (HEAD - 1)) == HS
+
+
+def linear_kernel(segments, shards, heads, prev, *refs):
+    refs = list(refs)
+    info, own, ups, downs = refs[0], refs[1], refs[2:5], refs[5:8]
+    states = refs[8 : 8 + len(segments)]
+    refs = refs[8 + len(segments) :]
+    gain, taps, left, right, plus, weight, out_weight = refs[:7]
+    refs = refs[7:]
+    if prev:
+        prev_key, prev_mixed, prev_value = refs[:3]
+        refs = refs[3:]
+    refs = refs[1:]
+    near, far, stay, key_out, mixed_out, value_out = refs[:6]
+    x, w, ow, q, k, m, y, sems, wsems = refs[6:]
+    width = heads * HEAD
+    total = x.shape[0]
+    plan = []
+    for segment, shard, row, rows in shards:
+        for here in range(4):
+            source = own if here == shard else (ups[here - shard - 1] if here > shard else downs[shard - here - 1])
+            plan.append(
+                (
+                    info[0] == here,
+                    source.at[info[4 + segment], pl.ds(0, rows)],
+                    x.at[pl.ds(row, rows)],
+                )
+            )
+    wait_x = copies(plan, sems)
+    weight_copy = pltpu.make_async_copy(weight, w, wsems.at[0])
+    out_copy = pltpu.make_async_copy(out_weight, ow, wsems.at[1])
+    weight_copy.start()
+    out_copy.start()
+    if prev:
+        k[pl.ds(0, prev), :] = prev_key[...]
+        m[pl.ds(0, prev), :] = prev_mixed[...]
+    wait_x()
+    weight_copy.wait()
+    tap = taps[...]
+    for number, (start, rows) in enumerate(segments):
+        base = prev if number == 0 else 0
+        tile = min(rows, 256)
+        if base:
+            ends = prev_value[...].astype(F32)
+            last2, last = ends[14:15], ends[15:16]
+        else:
+            ends = states[number][pl.ds(SQUARES + FD, 16), :].astype(F32)
+            last2, last = ends[1:2], ends[2:3]
+        for at in range(start, start + rows, tile):
+            normed = rms_norm(x[pl.ds(at, tile), :], gain[...])
+            q[pl.ds(at, tile), :] = dot(normed, w[:, :HEAD]).astype(BF)
+            k[pl.ds(prev + at, tile), :] = dot(normed, w[:, HEAD : 2 * HEAD]).astype(BF)
+            v = dot(normed, w[:, 2 * HEAD : 2 * HEAD + width]).astype(BF).astype(F32)
+            u = dot(normed, w[:, 2 * HEAD + width :]).astype(BF).astype(F32)
+            row = lax.broadcasted_iota(jnp.int32, v.shape, 0)
+            back1 = jnp.where(row == 0, last, pltpu.roll(v, 1, 0))
+            back2 = jnp.where(row == 0, last2, jnp.where(row == 1, last, pltpu.roll(v, 2, 0)))
+            last2, last = v[tile - 2 : tile - 1], v[tile - 1 : tile]
+            convolved = tap[0:1] * v + tap[1:2] * back1 + tap[2:3] * back2
+            mixed = convolved * (u / (1.0 + jnp.exp(-u)))
+            m[pl.ds(prev + at, tile), :] = jnp.where(lane_of_ones(v.shape), 1.0, mixed).astype(BF)
+            if number == 0 and at + tile == start + rows:
+                value_out[...] = v[tile - 16 :].astype(BF)
+    out_copy.wait()
+    for number, (start, rows) in enumerate(segments):
+        base = prev if number == 0 else 0
+        tile = min(rows, 256)
+        first = 0 if number == 0 else prev + start
+        for at in range(start, start + rows, tile):
+            queries = q[pl.ds(at, tile), :]
+            lane = lax.broadcasted_iota(jnp.int32, queries.shape, 1)
+            for head in range(heads):
+                columns = pl.ds(head * HEAD, HEAD)
+                mapped = (
+                    (dot(queries, left[head]) + plus[0:1, :])
+                    * (dot(queries, right[head]) + plus[1:2, :])
+                    * plus[2:3, :]
+                )
+                total_rows = dot(mapped.astype(BF), states[number][pl.ds(0, FEATURES), columns])
+                own_lanes = (lane >= head * FD) & (lane < (head + 1) * FD)
+                masked = jnp.where(own_lanes, queries, jnp.zeros_like(queries))
+                for key_at in range(first, prev + at + tile, tile):
+                    a = dot_t(masked, k[pl.ds(key_at, tile), :]) * FD ** (-0.5)
+                    weights = 1.0 + a + 0.5 * a * a
+                    if key_at == prev + at:
+                        causal = lax.broadcasted_iota(jnp.int32, a.shape, 0) >= lax.broadcasted_iota(
+                            jnp.int32, a.shape, 1
+                        )
+                        weights = jnp.where(causal, weights, 0.0)
+                    total_rows += dot(weights.astype(BF), m[pl.ds(key_at, tile), columns])
+                y[pl.ds(at, tile), columns] = (total_rows / total_rows[:, HS : HS + 1]).astype(BF)
+    key_out[...] = k[pl.ds(prev, key_out.shape[0]), :]
+    mixed_out[...] = m[pl.ds(prev, mixed_out.shape[0]), :]
+    pieces, _ = half_pieces(segments)
+    plan = []
+    for low in (0, 1):
+        for natural, rows, at in pieces[1 - low]:
+            plan.append((info[1] == low, x.at[pl.ds(natural, rows)], stay.at[pl.ds(at, rows)]))
+    copies(plan, sems)()
+    for start, rows in segments:
+        tile = min(rows, 256)
+        for at in range(start, start + rows, tile):
+            x[pl.ds(at, tile), :] = dot(y[pl.ds(at, tile), :], ow[...]).astype(BF)
+    put_halves(segments, info, x, near, far, sems)
+
+
+def window_kernel(segments, heads, prev, *refs):
+    refs = list(refs)
+    info, own, own_out, other, other_out = refs[:5]
+    states = refs[5 : 5 + len(segments)]
+    refs = refs[5 + len(segments) :]
+    gain, weight, out_weight = refs[:3]
+    refs = refs[3:]
+    if prev:
+        prev_keys, prev_values = refs[:2]
+        refs = refs[2:]
+    refs = refs[1:]
+    near, far, top, key_out, value_out = refs[:5]
+    x, w, ow, q, k, v, y, sems, wsems = refs[5:]
+    width = heads * HEAD
+    wait_x = copies(halves_plan(segments, info, own, own_out, other, other_out, x), sems)
+    weight_copy = pltpu.make_async_copy(weight, w, wsems.at[0])
+    out_copy = pltpu.make_async_copy(out_weight, ow, wsems.at[1])
+    weight_copy.start()
+    out_copy.start()
+    wait_x()
+    weight_copy.wait()
+    best = []
+    for number, (start, rows) in enumerate(segments):
+        shift = WIN * (number + 1)
+        if prev and number == 0:
+            k[pl.ds(0, WIN), :] = prev_keys[...]
+            v[pl.ds(0, WIN), :] = prev_values[...]
+        else:
+            old = states[number][pl.ds(STATE_VALUES, WIN), :]
+            k[pl.ds(start + shift - WIN, WIN), :] = states[number][pl.ds(STATE_KEYS, WIN), :]
+            v[pl.ds(start + shift - WIN, WIN), :] = jnp.where(
+                lane_of_ones(old.shape), jnp.ones_like(old), old
+            )
+        tile = min(rows, 256)
+        for at in range(start, start + rows, tile):
+            normed = rms_norm(x[pl.ds(at, tile), :], gain[...])
+            q[pl.ds(at, tile), :] = dot(normed, w[:, :width]).astype(BF)
+            k[pl.ds(shift + at, tile), :] = dot(normed, w[:, width : 2 * width]).astype(BF)
+            values = dot(normed, w[:, 2 * width :])
+            v[pl.ds(shift + at, tile), :] = jnp.where(lane_of_ones(values.shape), 1.0, values).astype(BF)
+        final = info[6 + number] - 1
+        tile = min(rows, 128)
+        best_here = jnp.full((1, 1), -jnp.inf, F32)
+        for at in range(start, start + rows, tile):
+            keys_here = tile + WIN
+            row = lax.broadcasted_iota(jnp.int32, (tile, keys_here), 0)
+            place = lax.broadcasted_iota(jnp.int32, (tile, keys_here), 1)
+            allowed = (place > row) & (place <= row + WIN)
+            for head in range(heads):
+                columns = pl.ds(head * HEAD, HEAD)
+                e = dot_t(q[pl.ds(at, tile), columns], k[pl.ds(shift - WIN + at, keys_here), columns])
+                e = jnp.where(allowed, e * HS ** (-0.5), -jnp.inf)
+                row_max = jnp.max(e, axis=-1, keepdims=True)
+                chances = jnp.exp(e - row_max).astype(BF)
+                o = dot(chances, v[pl.ds(shift - WIN + at, keys_here), columns])
+                y[pl.ds(at, tile), columns] = (o / o[:, HS : HS + 1]).astype(BF)
+                at_final = lax.broadcasted_iota(jnp.int32, row_max.shape, 0) + (at - start) == final
+                best_here = jnp.maximum(
+                    best_here, jnp.max(jnp.where(at_final, row_max, -jnp.inf), axis=0, keepdims=True)
+                )
+        best.append(best_here)
+    end = segments[0][1]
+    key_out[...] = k[pl.ds(end, WIN), :]
+    value_out[...] = v[pl.ds(end, WIN), :]
+    for number in range(len(segments)):
+        top[pl.ds(number * 8, 8), :] = jnp.broadcast_to(best[number], (8, 128))
+    out_copy.wait()
+    for start, rows in segments:
+        tile = min(rows, 256)
+        for at in range(start, start + rows, tile):
+            x[pl.ds(at, tile), :] = dot(y[pl.ds(at, tile), :], ow[...]).astype(BF)
+    put_halves(segments, info, x, near, far, sems)
+
+
+def hidden_kernel(segments, info, own, own_out, other, other_out, gain, gate, up, down, dep, near, far, x, n, total, sems):
+    step = pl.program_id(0)
+    rows = x.shape[0]
+    tile = rows if rows < 512 else rows // 2
+
+    @pl.when(step == 0)
+    def _():
+        copies(halves_plan(segments, info, own, own_out, other, other_out, x), sems)()
+        for at in range(0, rows, tile):
+            n[pl.ds(at, tile), :] = rms_norm(x[pl.ds(at, tile), :], gain[...])
+
+    for at in range(0, rows, tile):
+        normed = n[pl.ds(at, tile), :]
+        opened = dot(normed, gate[...])
+        inner = (opened / (1.0 + jnp.exp(-opened)) * dot(normed, up[...])).astype(BF)
+        part = dot(inner, down[...])
+
+        @pl.when(step == 0)
+        def _(at=at, part=part):
+            total[pl.ds(at, tile), :] = part
+
+        @pl.when(step > 0)
+        def _(at=at, part=part):
+            total[pl.ds(at, tile), :] += part
+
+    @pl.when(step == pl.num_programs(0) - 1)
+    def _():
+        for at in range(0, rows, tile):
+            x[pl.ds(at, tile), :] = total[pl.ds(at, tile), :].astype(BF)
+        put_halves(segments, info, x, near, far, sems)
+
+
+def call(body, outs, specs, scratch, operands, flops, moved, limit, grid=None):
+    return pl.pallas_call(
+        body,
+        grid=grid or (),
+        out_shape=[jax.ShapeDtypeStruct(shape, dtype) for shape, dtype, _ in outs],
+        in_specs=specs,
+        out_specs=[spec for _, _, spec in outs],
+        scratch_shapes=scratch,
+        compiler_params=pltpu.CompilerParams(vmem_limit_bytes=limit * MIB),
+        cost_estimate=pl.CostEstimate(flops=flops, bytes_accessed=moved, transcendentals=0),
+    )(*operands)
+
+
+def run_linear(segments, shards, heads, prev, info, own, ups, downs, states, consts, weights, before, dep):
+    total = sum(rows for _, rows in segments)
+    width = heads * HEAD
+    gain, taps, weight, out_weight = weights
+    half = (total // 2, D)
+    scratch = [
+        pltpu.VMEM((total, D), BF),
+        pltpu.VMEM(weight.shape, BF),
+        pltpu.VMEM(out_weight.shape, BF),
+        pltpu.VMEM((total, HEAD), BF),
+        pltpu.VMEM((prev + total, HEAD), BF),
+        pltpu.VMEM((prev + total, width), BF),
+        pltpu.VMEM((total, width), BF),
+        pltpu.SemaphoreType.DMA((20,)),
+        pltpu.SemaphoreType.DMA((2,)),
+    ]
+    rows = segments[0][1]
+    outs = [(half, BF, ANY)] * 3 + [((rows, HEAD), BF, VMEM), ((rows, width), BF, VMEM), ((16, width), BF, VMEM)]
+    operands = [info, own, *ups, *downs, *states, gain, taps, *consts, weight, out_weight, *before, dep]
+    specs = [SMEM] + [ANY] * 7 + [VMEM] * (len(states) + 2 + 3) + [ANY] * 2 + [VMEM] * len(before) + [ANY]
+    return call(
+        functools.partial(linear_kernel, segments, shards, heads, prev),
+        outs, specs, scratch, operands, 2 * total * D * 1792, 12 * MIB, 40,
+    )
+
+
+def run_window(segments, heads, prev, info, parts, states, weights, before, dep):
+    total = sum(rows for _, rows in segments)
+    width = heads * HEAD
+    gain, weight, out_weight = weights
+    half = (total // 2, D)
+    scratch = [
+        pltpu.VMEM((total, D), BF),
+        pltpu.VMEM(weight.shape, BF),
+        pltpu.VMEM(out_weight.shape, BF),
+        pltpu.VMEM((total, width), BF),
+        pltpu.VMEM((total + WIN * len(segments), width), BF),
+        pltpu.VMEM((total + WIN * len(segments), width), BF),
+        pltpu.VMEM((total, width), BF),
+        pltpu.SemaphoreType.DMA((20,)),
+        pltpu.SemaphoreType.DMA((2,)),
+    ]
+    outs = [(half, BF, ANY)] * 2 + [((8 * len(segments), 128), F32, VMEM)] + [((WIN, width), BF, VMEM)] * 2
+    operands = [info, *parts, *states, gain, weight, out_weight, *before, dep]
+    specs = [SMEM] + [ANY] * 4 + [VMEM] * (len(states) + 1) + [ANY] * 2 + [VMEM] * len(before) + [ANY]
+    return call(
+        functools.partial(window_kernel, segments, heads, prev),
+        outs, specs, scratch, operands, 2 * total * D * 2048, 12 * MIB, 40,
+    )
+
+
+def run_hidden(segments, info, parts, weights, dep):
+    total = sum(rows for _, rows in segments)
+    gain, gate, up, down = weights
+    half = (total // 2, D)
+    units = gate.shape[1]
+    block = 256
+    specs = [SMEM] + [ANY] * 4 + [
+        pl.BlockSpec((1, D), lambda i: (0, 0)),
+        pl.BlockSpec((D, block), lambda i: (0, i)),
+        pl.BlockSpec((D, block), lambda i: (0, i)),
+        pl.BlockSpec((block, D), lambda i: (i, 0)),
+        ANY,
+    ]
+    scratch = [
+        pltpu.VMEM((total, D), BF),
+        pltpu.VMEM((total, D), BF),
+        pltpu.VMEM((total, D), F32),
+        pltpu.SemaphoreType.DMA((20,)),
+    ]
+    return call(
+        functools.partial(hidden_kernel, segments),
+        [(half, BF, ANY)] * 2, specs, scratch, [info, *parts, gain, gate, up, down, dep],
+        2 * total * D * units * 3, 24 * MIB, 40, (units // block,),
+    )
+
+
+INWARD, ACROSS, OUTWARD = [(0, 1), (3, 2)], [(1, 2), (2, 1)], [(1, 0), (2, 3)]
+
+
+def to_middle(near, far, stay):
+    far_in = lax.ppermute(far, "tensor", INWARD)
+    near_in = lax.ppermute(near, "tensor", INWARD)
+    crossed = lax.ppermute(far + far_in, "tensor", ACROSS)
+    return (stay.astype(F32) + (near.astype(F32) + near_in.astype(F32) + crossed.astype(F32))).astype(BF)
+
+
+def from_middle(own):
+    other = lax.ppermute(own, "tensor", ACROSS)
+    own_out = lax.ppermute(own, "tensor", OUTWARD)
+    other_out = lax.ppermute(other, "tensor", OUTWARD)
+    return own, own_out, other, other_out
+
+
+def pick_axis(array, axis, index):
+    return jnp.where(index, lax.index_in_dim(array, 1, axis, False), lax.index_in_dim(array, 0, axis, False))
+
+
+def slot_states(request_group, group_slot, sums, norms, keys, values, tail, count):
+    here = lax.axis_index("req")
+    slots_here, heads = sums.shape[:2]
+    width = heads * HEAD
+    requests = request_group.shape[0]
+    groups = lax.all_gather(request_group, "req", axis=0, tiled=True)
+    matches = jnp.arange(group_slot.shape[0])[None, :] == groups[:, None]
+    slots = jnp.sum(jnp.where(matches, group_slot[None, :], 0), axis=1)
+
+    def padded(rows):
+        rows = rows.reshape(slots_here, rows.shape[1], heads, HS)
+        return jnp.pad(rows, ((0, 0), (0, 0), (0, 0), (0, HEAD - HS))).reshape(slots_here, -1, width)
+
+    fold = jnp.asarray(fold_matrix())
+    folded = jnp.einsum("fg,ahgd->afhd", fold, sums, precision=lax.Precision.HIGHEST)
+    folded_norms = jnp.einsum("fg,ahg->afh", fold, norms, precision=lax.Precision.HIGHEST)
+    folded = jnp.concatenate([folded, folded_norms[..., None]], axis=-1).astype(BF)
+    folded = jnp.pad(folded, ((0, 0), (0, 0), (0, 0), (0, HEAD - HS - 1))).reshape(slots_here, -1, width)
+    gap = jnp.zeros((slots_here, STATE_KEYS - SQUARES - FD - 1 - (KC - 1), width), BF)
+    pack = jnp.concatenate([folded, padded(tail), gap, padded(keys), padded(values)], axis=1)
+
+    bits = []
+    while 1 << len(bits) < count:
+        bits.append(len(bits))
+    local = (slots - here * slots_here).reshape((2,) * len(bits) + (requests,))
+
+    def chosen(places):
+        flat = places.reshape(-1)
+        owned = (flat >= 0) & (flat < slots_here)
+        rows = jnp.take(pack, jnp.clip(flat, 0, slots_here - 1), axis=0)
+        rows = jnp.where(owned[:, None, None], rows, jnp.zeros_like(rows))
+        return rows.reshape(places.shape + rows.shape[1:])
+
+    def swap(array, bit):
+        return lax.ppermute(array, "req", [(i, i ^ (1 << bit)) for i in range(count)])
+
+    def upper(bit):
+        return (here >> bit) & 1 == 1
+
+    axis = len(bits) - 1
+    packs = chosen(pick_axis(local, axis, upper(0))) + swap(chosen(pick_axis(local, axis, ~upper(0))), 0)
+    halves = []
+    cut = STATE_ROWS // 2
+    for number in range(2):
+        part = packs[..., number * cut : (number + 1) * cut, :]
+        left = bits[1:]
+        order = left if number == 0 else left[::-1]
+        while order:
+            bit, order = order[0], order[1:]
+            axis = len(left) - 1 - left.index(bit)
+            left = [b for b in left if b != bit]
+            part = pick_axis(part, axis, upper(bit)) + swap(pick_axis(part, axis, ~upper(bit)), bit)
+        halves.append(part)
+    return jnp.concatenate(halves, axis=1)
+
+
+def make_line(req_count):
+    def per_device(
+        hidden,
+        suffix_len,
+        request_group,
+        group_slot,
+        norm_first,
+        query_weight,
+        key_weight,
+        value_weight,
+        filter_gate,
+        filter_taps,
+        linear_out,
+        norm_second,
+        window_query,
+        window_key,
+        window_value,
+        window_out,
+        norm_third,
+        gate_weight,
+        up_weight,
+        down_weight,
+        prefix_sums,
+        prefix_norms,
+        prefix_keys,
+        prefix_values,
+        prefix_tail,
+    ):
+        requests = hidden.shape[0]
+        heads = prefix_sums.shape[1]
+        share = hidden.shape[1]
+        here = lax.axis_index("tensor")
+        low = here < 2
+        middle = (here == 1) | (here == 2)
+
+        ups, downs = [], []
+        up = down = hidden
+        for step in range(1, 4):
+            up = lax.ppermute(up, "tensor", [(i, i + 1) for i in range(step - 1, 3)])
+            down = lax.ppermute(down, "tensor", [(i + 1, i) for i in range(4 - step)])
+            ups.append(up)
+            downs.append(down)
+        states = slot_states(
+            request_group, group_slot, prefix_sums, prefix_norms, prefix_keys, prefix_values, prefix_tail, req_count
+        )
+
+        def wide(matrix):
+            matrix = matrix.reshape(matrix.shape[0], heads, HS)
+            return jnp.pad(matrix, ((0, 0), (0, 0), (0, HEAD - HS))).reshape(matrix.shape[0], heads * HEAD)
+
+        def tall(matrix):
+            matrix = matrix.reshape(heads, HS, matrix.shape[1])
+            return jnp.pad(matrix, ((0, 0), (0, HEAD - HS), (0, 0))).reshape(heads * HEAD, -1)
+
+        def lanes(matrix):
+            return jnp.pad(matrix, ((0, 0), (0, HEAD - matrix.shape[1])))
+
+        linear_weights = (
+            norm_first[None],
+            jnp.pad(wide(filter_taps), ((0, 8 - KC), (0, 0))),
+            jnp.concatenate(
+                [lanes(query_weight), lanes(key_weight), wide(value_weight), wide(filter_gate)], axis=1
+            ),
+            tall(linear_out),
+        )
+        window_weights = (
+            norm_second[None],
+            jnp.concatenate([wide(window_query), wide(window_key), wide(window_value)], axis=1),
+            tall(window_out),
+        )
+        hidden_weights = (norm_third[None], gate_weight, up_weight, down_weight)
+        left, right, plus = feature_maps(heads)
+        consts = (jnp.asarray(left, BF), jnp.asarray(right, BF), jnp.asarray(plus))
+
+        place = [here, low.astype(jnp.int32), middle.astype(jnp.int32), here * 0]
+        segments = ((0, LMAX),)
+        shards = tuple((0, s, s * share, share) for s in range(4))
+        infos, own, parts, tops = [], [], [], []
+        for request in range(requests):
+            infos.append(
+                jnp.stack(place + [here * 0 + request, here * 0, suffix_len[request], here * 0]).astype(jnp.int32)
+            )
+        dep = hidden
+        for request in range(requests):
+            near, far, stay, *_ = run_linear(
+                segments, shards, heads, 0, infos[request], hidden, ups, downs,
+                [states[request]], consts, linear_weights, [], dep,
+            )
+            own.append(to_middle(near, far, stay))
+            dep = own[-1]
+        for request in range(requests):
+            parts.append(from_middle(own[request]))
+        for request in range(requests):
+            near, far, top, *_ = run_window(
+                segments, heads, 0, infos[request], parts[request], [states[request]], window_weights, [], dep
+            )
+            own[request] = to_middle(near, far, own[request])
+            dep = own[request]
+            tops.append(top[0, 0])
+        for request in range(requests):
+            parts[request] = from_middle(own[request])
+        for request in range(requests):
+            near, far = run_hidden(segments, infos[request], parts[request], hidden_weights, dep)
+            own[request] = to_middle(near, far, own[request])
+            dep = own[request]
+        outs, squares = [], []
+        rows_here = here * share + jnp.arange(share)
+        for request in range(requests):
+            first, second = own[request][:share], own[request][share:]
+            moved = lax.ppermute(jnp.where(low, first, second), "tensor", OUTWARD)
+            mine = jnp.where(middle, jnp.where(low, second, first), moved)
+            live = (rows_here < suffix_len[request])[:, None]
+            outs.append(jnp.where(live, mine, jnp.zeros_like(mine)))
+            floats = mine.astype(F32)
+            squares.append(jnp.sum(jnp.where(live, floats * floats, 0.0)))
+        scalars = jnp.stack(squares + tops)
+        scalars = jnp.broadcast_to(scalars[:, None], (2 * requests, 128))
+        everyone = [scalars] + [
+            lax.ppermute(scalars, "tensor", [(i, (i + step) % 4) for i in range(4)]) for step in (1, 2, 3)
+        ]
+        total = sum(each[:requests, 0] for each in everyone)
+        top_logit = functools.reduce(jnp.maximum, [each[requests:, 0] for each in everyone])
+        return jnp.stack(outs), jnp.sqrt(total / D), top_logit
+
+    return per_device
 
 
 def folded_features(queries):
@@ -34,7 +647,7 @@
     return jnp.concatenate(parts, axis=-1)
 
 
-def fold_matrix():
+def plain_fold_matrix():
     row = jnp.arange(1 + FD + PAIRS * FD)[:, None]
     column = jnp.arange(1 + FD + FD * FD)[None, :]
     shift, first = (row - 1 - FD) // FD, (row - 1 - FD) % FD
@@ -78,34 +691,7 @@
     return block(here).astype(F32) + up.astype(F32) + down.astype(F32)
 
 
-def middle_exchange(partial, stream, axis):
-    here = lax.axis_index(axis)
-    half = partial.shape[0] // 2
-    low = here < 2
-    middle = (here == 1) | (here == 2)
-
-    def near_far(rows):
-        first, second = rows[:half], rows[half:]
-        return jnp.where(low, first, second), jnp.where(low, second, first)
-
-    inward, across, outward = [(0, 1), (3, 2)], [(1, 2), (2, 1)], [(1, 0), (2, 3)]
-    near, far = near_far(partial)
-    far_in = lax.ppermute(far, axis, inward)
-    near_in = lax.ppermute(near, axis, inward)
-    crossed = lax.ppermute(far + far_in, axis, across)
-    total = near.astype(F32) + near_in.astype(F32) + crossed.astype(F32)
-    own = (near_far(stream)[0].astype(F32) + total).astype(BF)
-    other = lax.ppermute(own, axis, across)
-    own_out = lax.ppermute(own, axis, outward)
-    other_out = lax.ppermute(other, axis, outward)
-    near = jnp.where(middle, own, own_out)
-    far = jnp.where(middle, other, other_out)
-    return jnp.concatenate([jnp.where(low, near, far), jnp.where(low, far, near)])
-
-
 def settle(partial, stream, axis, count):
-    if count == 4:
-        return middle_exchange(partial, stream, axis)
     here = lax.axis_index(axis)
     size = partial.shape[0] // count
     mine = lax.dynamic_slice_in_dim(stream, here * size, size, 0)
@@ -126,7 +712,7 @@
     return packs[0]
 
 
-def make(req_count, tensor_count):
+def make_plain(req_count, tensor_count):
     def per_device(
         hidden,
         suffix_len,
@@ -162,7 +748,7 @@
         groups = lax.all_gather(request_group, "req", axis=0, tiled=True)
         matches = jnp.arange(group_slot.shape[0])[None, :] == groups[:, None]
         slots = jnp.sum(jnp.where(matches, group_slot[None, :], 0), axis=1)
-        fold = fold_matrix()
+        fold = plain_fold_matrix()
         sums = jnp.einsum("fg,ahgd->afhd", fold, prefix_sums, precision=lax.Precision.HIGHEST)
         terms = sums.shape[1]
         norms = jnp.einsum("fg,ahg->afh", fold, prefix_norms, precision=lax.Precision.HIGHEST)
@@ -290,7 +876,7 @@
 
 def solution(mesh):
     return jax.shard_map(
-        make(mesh.shape["req"], mesh.shape["tensor"]),
+        make_line(mesh.shape["req"]) if mesh.shape["tensor"] == 4 else make_plain(mesh.shape["req"], mesh.shape["tensor"]),
         mesh=mesh,
         in_specs=(
             P("req", "tensor", None),

time: 718 us -> 529 us (0.74)
  matrix products: 107 us -> 4.79 us
  Pallas kernels: 0 us -> 90.7 us
  waiting for transfers between devices: 288 us -> 228 us
  local copies, waits for them, and re-layouts: 123 us -> 68.4 us
  other arithmetic: 71.6 us -> 42.1 us
  starting transfers between devices: 88 us -> 73.4 us
  blocking collectives: 23 us -> 9.46 us
    dot_general x34 -> x2, matrix products: 107 us -> 4.79 us  [the longest x1 3.41 us: slot_states(): jnp.einsum('fg,ahgd->afhd', fold, sums, precision=lax.Precision.HIGHEST)]
    pallas_call x0 -> x6, Pallas kernels: none -> 90.7 us  [call(): pl.pallas_call(body, grid=grid or (), out_shape=[jax.ShapeDtypeStruct(sha...]
    ppermute x51 -> x46, waiting for transfers between devices: 288 us -> 228 us  [the longest x6 58.2 us: to_middle(): far_in = lax.ppermute(far, 'tensor', INWARD)]
    slice x57 -> x2, local copies, waits for them, and re-layouts: 43.3 us -> 1.03 us  [per_device(): tops.append(top[0, 0])]
    concatenate x5 -> x2, local copies, waits for them, and re-layouts: 34.6 us -> 0.99 us  [the longest x1 0.66 us: slot_states(): jnp.concatenate([folded, padded(tail), gap, padded(keys), padded(values)]...]
    ppermute x51 -> x46, starting transfers between devices: 88 us -> 73.4 us  [the longest x6 16.7 us: to_middle(): near_in = lax.ppermute(near, 'tensor', INWARD)]
    pad x1 -> x12, local copies, waits for them, and re-layouts: 0.01 us -> 14 us  [the longest x5 11.7 us: wide(): jnp.pad(matrix, ((0, 0), (0, 0), (0, HEAD - HS)))]
    unnamed x2 -> x1, blocking collectives: 23 us -> 9.46 us
  transfers between devices with their start and end apart: 51 -> 46, of which waited for: 25 -> 27; matrix products, arithmetic and copies ran while one was open for 30% -> 13% of each run, Pallas kernels for 0% -> 0%
where the time goes in v2:
time: 529 us; the launch traced here: 519 us
  waiting for transfers between devices  228 us (43%)
  Pallas kernels  90.7 us (17%)
  starting transfers between devices  73.4 us (14%)
  local copies, waits for them, and re-layouts  68.4 us (13%)
  other arithmetic  42.1 us (8%)
  blocking collectives  9.46 us (2%)
    pallas_call x6, Pallas kernels, call(): pl.pallas_call(body, grid=grid or (), out_shape=[jax.ShapeDtypeStruct(sha...  90.7 us
    ppermute x6, waiting for transfers between devices, to_middle(): far_in = lax.ppermute(far, 'tensor', INWARD)  58.2 us
    ppermute x4, waiting for transfers between devices, from_middle(): other_out = lax.ppermute(other, 'tensor', OUTWARD)  42 us
    ppermute x6, waiting for transfers between devices, to_middle(): near_in = lax.ppermute(near, 'tensor', INWARD)  39.7 us
    ppermute x4, waiting for transfers between devices, from_middle(): own_out = lax.ppermute(own, 'tensor', OUTWARD)  38.6 us
    unnamed x80, local copies, waits for them, and re-layouts  23.8 us
    ppermute x3, waiting for transfers between devices, per_device(): down = lax.ppermute(down, 'tensor', [(i + 1, i) for i in range(4 - step)])  21.5 us
    ppermute x2, waiting for transfers between devices, per_device(): moved = lax.ppermute(jnp.where(low, first, second), 'tensor', OUTWARD)  20.1 us
  transfers between devices with their start and end apart: 46, of which 27 were waited for; matrix products, arithmetic and copies ran while one was open for 13% of the time, Pallas kernels for 0%

profile of v2, /device:TPU:0, one launch (start us, length us, event | category | flops | bytes accessed | tf_op | source)
XLA Modules:
  0.0 519.1 jit_solution(9321355319585413746)
XLA Ops:
  3.6 9.5 %all-reduce.15 = s32[16]{0:T(128)S(1)} all-reduce(s32[16]{0:T(128)S(1)} %dynamic-update-slice), channel_id=1, replica_groups=mesh['req'=8,'tensor'=4] {'req'}, use_global_device_ids=true, to_apply=%add.15 | all-reduce | flops 16 | bytes 128
  28.3 4.5 collective-permute-start
  70.5 12.9 %collective-permute-done.4.refs_6_ = bf16[2,128,1792]{2,1,0:T(8,128)(2,1)} collective-permute-done((bf16[2,128,1792]{2,1,0:T(8,128)(2,1)}, bf16[2,128,1792]{2,1,0:T(8,128)(2,1)}, u32[]{:S(2)}, u32[]{:S(2)}) %collective-permute-start.4) | collective-permute-done | bytes 917536 | tf_op jit(solution)/shard_map/ppermute | solution.py:554
  91.4 5.2 %collective-permute-done.10 = bf16[2,152,512]{2,1,0:T(8,128)(2,1)} collective-permute-done((bf16[2,152,512]{2,1,0:T(8,128)(2,1)}, bf16[2,152,512]{2,1,0:T(8,128)(2,1)}, u32[]{:S(2)}, u32[]{:S(2)}) %collective-permute-start.10) | collective-permute-done | bytes 311328 | tf_op jit(solution)/shard_map/ppermute | solution.py:493
  99.1 7.9 %collective-permute-done.5.refs_7_ = bf16[2,128,1792]{2,1,0:T(8,128)(2,1)} collective-permute-done((bf16[2,128,1792]{2,1,0:T(8,128)(2,1)}, bf16[2,128,1792]{2,1,0:T(8,128)(2,1)}, u32[]{:S(2)}, u32[]{:S(2)}) %collective-permute-start.5) | collective-permute-done | bytes 917536 | tf_op jit(solution)/shard_map/ppermute | solution.py:554
  107.0 13.4 %shard_map.292 = (bf16[256,1792]{1,0:T(8,128)(2,1)}, bf16[256,1792]{1,0:T(8,128)(2,1)S(1)}, bf16[256,1792]{1,0:T(8,128)(2,1)S(1)}, bf16[512,128]{1,0:T(8,128)(2,...) custom-call(s32[8]{0:T(128)S(1)} %stack.51.refs_0_.info, bf16[2,128,1792]{2,1,0:T(8,128)(2,1)S(1)} %copy-done.2, ...), custom_call_target="tpu_custom_call" | custom-call | flops 3288334336 | bytes 12582912 | tf_op jit(solution)/shard_map/pallas_call | solution.py:349
  124.9 18.5 %collective-permute-done.12 = bf16[256,1792]{1,0:T(8,128)(2,1)S(1)} collective-permute-done((bf16[256,1792]{1,0:T(8,128)(2,1)S(1)}, bf16[256,1792]{1,0:T(8,128)(2,1)S(1)}, u32[]{:S(2)}, u32[]{:S(2)}) %collective-permute-start.12) | collective-permute-done | bytes 917536 | tf_op jit(solution)/shard_map/ppermute | solution.py:442
  146.9 13.7 %collective-permute-done.11 = bf16[256,1792]{1,0:T(8,128)(2,1)} collective-permute-done((bf16[256,1792]{1,0:T(8,128)(2,1)}, bf16[256,1792]{1,0:T(8,128)(2,1)}, u32[]{:S(2)}, u32[]{:S(2)}) %collective-permute-start.11) | collective-permute-done | bytes 917536 | tf_op jit(solution)/shard_map/ppermute | solution.py:443
  163.1 13.7 %shard_map.293 = (bf16[256,1792]{1,0:T(8,128)(2,1)S(1)}, bf16[256,1792]{1,0:T(8,128)(2,1)}, bf16[256,1792]{1,0:T(8,128)(2,1)S(1)}, bf16[512,128]{1,0:T(8,128)(2,...) custom-call(s32[8]{0:T(128)S(1)} %stack.52.refs_0_.info, bf16[2,128,1792]{2,1,0:T(8,128)(2,1)S(1)} %copy-done.2, ...), custom_call_target="tpu_custom_call" | custom-call | flops 3288334336 | bytes 12582912 | tf_op jit(solution)/shard_map/pallas_call | solution.py:349
  178.8 8.6 %collective-permute-start.18 = (bf16[256,1792]{1,0:T(8,128)(2,1)}, bf16[256,1792]{1,0:T(8,128)(2,1)}, u32[]{:S(2)}, u32[]{:S(2)}) collective-permute-start(bf16[256,1792]{1,0:T(8,128)(2,1)} %get-tuple-element.25), channel_id=1, source_target_pairs={{0,1},{3,2},{4,5},{7,6},{8,9},{11,10},{12,13},{15,14},{16,17},{19,... | collective-permute-start | bytes 2752520 | tf_op jit(solution)/shard_map/ppermute | solution.py:442
  218.3 5.6 %collective-permute-done.17 = bf16[256,1792]{1,0:T(8,128)(2,1)S(1)} collective-permute-done((bf16[256,1792]{1,0:T(8,128)(2,1)S(1)}, bf16[256,1792]{1,0:T(8,128)(2,1)S(1)}, u32[]{:S(2)}, u32[]{:S(2)}) %collective-permute-start.17) | collective-permute-done | bytes 917536 | tf_op jit(solution)/shard_map/ppermute | solution.py:443
  224.5 13.5 %collective-permute-done.14.refs_2_ = bf16[256,1792]{1,0:T(8,128)(2,1)S(1)} collective-permute-done((bf16[256,1792]{1,0:T(8,128)(2,1)S(1)}, bf16[256,1792]{1,0:T(8,128)(2,1)S(1)}, u32[]{:S(2)}, u32[]{:S(2)}) %collective-permute-start.14) | collective-permute-done | bytes 917536 | tf_op jit(solution)/shard_map/ppermute | solution.py:450
  238.0 12.5 %collective-permute-done.16.refs_4_ = bf16[256,1792]{1,0:T(8,128)(2,1)S(1)} collective-permute-done((bf16[256,1792]{1,0:T(8,128)(2,1)S(1)}, bf16[256,1792]{1,0:T(8,128)(2,1)S(1)}, u32[]{:S(2)}, u32[]{:S(2)}) %collective-permute-start.16) | collective-permute-done | bytes 917536 | tf_op jit(solution)/shard_map/ppermute | solution.py:451
  253.1 11.2 %shard_map.294 = (bf16[256,1792]{1,0:T(8,128)(2,1)S(1)}, bf16[256,1792]{1,0:T(8,128)(2,1)S(1)}, f32[8,128]{1,0:T(8,128)S(1)}, bf16[64,512]{1,0:T(8,128)(2,1)}, bf16[64,512]{1,0:T(8,128)(2,1)}) custom-call(s32[8]{0:T(128)S(1)} %stack.51.refs_0_.info, bf16[256,1792]{1,0:T(8,128)(2,1)S(1)} %copy-done.4, bf16[256,1792]{1,0:T(8,128)(2,1)S(1)} %collective-permute-done.14.refs_2_, ...), custom_call_target="tpu_custom_call" | custom-call | flops 3758096384 | bytes 12582912 | tf_op jit(solution)/shard_map/pallas_call | solution.py:349
  270.7 15.8 %collective-permute-done.21 = bf16[256,1792]{1,0:T(8,128)(2,1)S(1)} collective-permute-done((bf16[256,1792]{1,0:T(8,128)(2,1)S(1)}, bf16[256,1792]{1,0:T(8,128)(2,1)S(1)}, u32[]{:S(2)}, u32[]{:S(2)}) %collective-permute-start.21) | collective-permute-done | bytes 917536 | tf_op jit(solution)/shard_map/ppermute | solution.py:442
  290.1 8.2 %collective-permute-done.20 = bf16[256,1792]{1,0:T(8,128)(2,1)S(1)} collective-permute-done((bf16[256,1792]{1,0:T(8,128)(2,1)S(1)}, bf16[256,1792]{1,0:T(8,128)(2,1)S(1)}, u32[]{:S(2)}, u32[]{:S(2)}) %collective-permute-start.20) | collective-permute-done | bytes 917536 | tf_op jit(solution)/shard_map/ppermute | solution.py:443
  298.7 9.1 %collective-permute-done.26.refs_2_ = bf16[256,1792]{1,0:T(8,128)(2,1)S(1)} collective-permute-done((bf16[256,1792]{1,0:T(8,128)(2,1)S(1)}, bf16[256,1792]{1,0:T(8,128)(2,1)S(1)}, u32[]{:S(2)}, u32[]{:S(2)}) %collective-permute-start.26) | collective-permute-done | bytes 917536 | tf_op jit(solution)/shard_map/ppermute | solution.py:450
  307.9 9.8 %collective-permute-done.28.refs_4_ = bf16[256,1792]{1,0:T(8,128)(2,1)S(1)} collective-permute-done((bf16[256,1792]{1,0:T(8,128)(2,1)S(1)}, bf16[256,1792]{1,0:T(8,128)(2,1)S(1)}, u32[]{:S(2)}, u32[]{:S(2)}) %collective-permute-start.28) | collective-permute-done | bytes 917536 | tf_op jit(solution)/shard_map/ppermute | solution.py:451
  320.3 11.4 %shard_map.295 = (bf16[256,1792]{1,0:T(8,128)(2,1)S(1)}, bf16[256,1792]{1,0:T(8,128)(2,1)S(1)}, f32[8,128]{1,0:T(8,128)S(1)}, bf16[64,512]{1,0:T(8,128)(2,1)}, bf16[64,512]{1,0:T(8,128)(2,1)}) custom-call(s32[8]{0:T(128)S(1)} %stack.52.refs_0_.info, bf16[256,1792]{1,0:T(8,128)(2,1)S(1)} %add_convert_fusion.4.refs_9_.refs_1_, ...), custom_call_target="tpu_custom_call" | custom-call | flops 3758096384 | bytes 12582912 | tf_op jit(solution)/shard_map/pallas_call | solution.py:349
  337.3 8.3 %collective-permute-done.30 = bf16[256,1792]{1,0:T(8,128)(2,1)S(1)} collective-permute-done((bf16[256,1792]{1,0:T(8,128)(2,1)S(1)}, bf16[256,1792]{1,0:T(8,128)(2,1)S(1)}, u32[]{:S(2)}, u32[]{:S(2)}) %collective-permute-start.30) | collective-permute-done | bytes 917536 | tf_op jit(solution)/shard_map/ppermute | solution.py:442
  349.2 6.2 %collective-permute-done.29 = bf16[256,1792]{1,0:T(8,128)(2,1)S(1)} collective-permute-done((bf16[256,1792]{1,0:T(8,128)(2,1)S(1)}, bf16[256,1792]{1,0:T(8,128)(2,1)S(1)}, u32[]{:S(2)}, u32[]{:S(2)}) %collective-permute-start.29) | collective-permute-done | bytes 917536 | tf_op jit(solution)/shard_map/ppermute | solution.py:443
  355.9 8.4 %collective-permute-done.23.own_out = bf16[256,1792]{1,0:T(8,128)(2,1)S(1)} collective-permute-done((bf16[256,1792]{1,0:T(8,128)(2,1)S(1)}, bf16[256,1792]{1,0:T(8,128)(2,1)S(1)}, u32[]{:S(2)}, u32[]{:S(2)}) %collective-permute-start.23) | collective-permute-done | bytes 917536 | tf_op jit(solution)/shard_map/ppermute | solution.py:450
  364.3 9.8 %collective-permute-done.25.other_out = bf16[256,1792]{1,0:T(8,128)(2,1)S(1)} collective-permute-done((bf16[256,1792]{1,0:T(8,128)(2,1)S(1)}, bf16[256,1792]{1,0:T(8,128)(2,1)S(1)}, u32[]{:S(2)}, u32[]{:S(2)}) %collective-permute-start.25) | collective-permute-done | bytes 917536 | tf_op jit(solution)/shard_map/ppermute | solution.py:451
  377.0 20.5 %shard_map.296 = (bf16[256,1792]{1,0:T(8,128)(2,1)S(1)}, bf16[256,1792]{1,0:T(8,128)(2,1)S(1)}) custom-call(s32[8]{0:T(128)S(1)} %stack.51.refs_0_.info, bf16[256,1792]{1,0:T(8,128)(2,1)S(1)} %add_convert_fusion.3.refs_9_.own, bf16[256,1792]{1,0:T(8,128)(2,1)S(1)} %collective-permute-done.23.own_out, bf16[256,1792]{1,0:T(8,128)(2,1)S(1)} %collective-permute-done.24.other, ...), custom_call_target="tpu_custom_call" | custom-call | flops 9865003008 | bytes 25165824 | tf_op jit(solution)/shard_map/pallas_call | solution.py:349
  402.8 7.0 %collective-permute-done.33 = bf16[256,1792]{1,0:T(8,128)(2,1)S(1)} collective-permute-done((bf16[256,1792]{1,0:T(8,128)(2,1)S(1)}, bf16[256,1792]{1,0:T(8,128)(2,1)S(1)}, u32[]{:S(2)}, u32[]{:S(2)}) %collective-permute-start.33) | collective-permute-done | bytes 917536 | tf_op jit(solution)/shard_map/ppermute | solution.py:442
  413.7 6.0 %collective-permute-done.32 = bf16[256,1792]{1,0:T(8,128)(2,1)S(1)} collective-permute-done((bf16[256,1792]{1,0:T(8,128)(2,1)S(1)}, bf16[256,1792]{1,0:T(8,128)(2,1)S(1)}, u32[]{:S(2)}, u32[]{:S(2)}) %collective-permute-start.32) | collective-permute-done | bytes 917536 | tf_op jit(solution)/shard_map/ppermute | solution.py:443
  420.2 7.6 %collective-permute-done.36.own_out = bf16[256,1792]{1,0:T(8,128)(2,1)S(1)} collective-permute-done((bf16[256,1792]{1,0:T(8,128)(2,1)S(1)}, bf16[256,1792]{1,0:T(8,128)(2,1)S(1)}, u32[]{:S(2)}, u32[]{:S(2)}) %collective-permute-start.36) | collective-permute-done | bytes 917536 | tf_op jit(solution)/shard_map/ppermute | solution.py:450
  427.8 9.8 %collective-permute-done.38.other_out = bf16[256,1792]{1,0:T(8,128)(2,1)S(1)} collective-permute-done((bf16[256,1792]{1,0:T(8,128)(2,1)S(1)}, bf16[256,1792]{1,0:T(8,128)(2,1)S(1)}, u32[]{:S(2)}, u32[]{:S(2)}) %collective-permute-start.38) | collective-permute-done | bytes 917536 | tf_op jit(solution)/shard_map/ppermute | solution.py:451
  440.4 20.5 %shard_map.297 = (bf16[256,1792]{1,0:T(8,128)(2,1)S(1)}, bf16[256,1792]{1,0:T(8,128)(2,1)S(1)}) custom-call(s32[8]{0:T(128)S(1)} %stack.52.refs_0_.info, bf16[256,1792]{1,0:T(8,128)(2,1)S(1)} %add_convert_fusion.2.dep.own, bf16[256,1792]{1,0:T(8,128)(2,1)S(1)} %collective-permute-done.36.own_out, bf16[256,1792]{1,0:T(8,128)(2,1)S(1)} %collective-permute-done.37.other, ...), custom_call_target="tpu_custom_call" | custom-call | flops 9865003008 | bytes 25165824 | tf_op jit(solution)/shard_map/pallas_call | solution.py:349
  464.7 8.6 %collective-permute-done.40 = bf16[256,1792]{1,0:T(8,128)(2,1)S(1)} collective-permute-done((bf16[256,1792]{1,0:T(8,128)(2,1)S(1)}, bf16[256,1792]{1,0:T(8,128)(2,1)S(1)}, u32[]{:S(2)}, u32[]{:S(2)}) %collective-permute-start.40) | collective-permute-done | bytes 917536 | tf_op jit(solution)/shard_map/ppermute | solution.py:442
  480.5 10.4 %collective-permute-done.35 = bf16[128,1792]{1,0:T(8,128)(2,1)S(1)} collective-permute-done((bf16[128,1792]{1,0:T(8,128)(2,1)}, bf16[128,1792]{1,0:T(8,128)(2,1)S(1)}, u32[]{:S(2)}, u32[]{:S(2)}) %collective-permute-start.35) | collective-permute-done | bytes 458784 | tf_op jit(solution)/shard_map/ppermute | solution.py:624
  495.3 9.7 %collective-permute-done.42 = bf16[128,1792]{1,0:T(8,128)(2,1)S(1)} collective-permute-done((bf16[128,1792]{1,0:T(8,128)(2,1)S(1)}, bf16[128,1792]{1,0:T(8,128)(2,1)S(1)}, u32[]{:S(2)}, u32[]{:S(2)}) %collective-permute-start.42) | collective-permute-done | bytes 458784 | tf_op jit(solution)/shard_map/ppermute | solution.py:624
  (242 shorter events, 178.5 us)
Async XLA Ops:
  28.3 30.2 %collective-permute-start.6 = (bf16[2,2,2,304,512]{4,3,2,1,0:T(8,128)(2,1)}, bf16[2,2,2,304,512]{4,3,2,1,0:T(8,128)(2,1)}, u32[]{:S(2)}, u32[]{:S(2)}) collective-permute-start(bf16[2,2,2,304,512]{4,3,2,1,0:T(8,128)(2,1)} %bitcast.12), channel_id=1, source_target_pairs={{0,4},{4,0},{8,12},{12,8},{16,20},{20,16},{24,28},{28,24},{1,5},{5... | collective-permute-start | bytes 7471112 | tf_op jit(solution)/shard_map/ppermute | solution.py:493
  28.3 26.6 %collective-permute-start = (bf16[2,128,1792]{2,1,0:T(8,128)(2,1)S(1)}, bf16[2,128,1792]{2,1,0:T(8,128)(2,1)}, u32[]{:S(2)}, u32[]{:S(2)}) collective-permute-start(bf16[2,128,1792]{2,1,0:T(8,128)(2,1)S(1)} %copy-done.2), channel_id=1, source_target_pairs={{0,1},{1,2},{2,3},{4,5},{5,6},{6,7},{8,9},{9,10},{10,11},{12,13},{... | collective-permute-start | bytes 2752520 | tf_op jit(solution)/shard_map/ppermute | solution.py:553
  32.8 24.5 %collective-permute-start.3 = (bf16[2,128,1792]{2,1,0:T(8,128)(2,1)S(1)}, bf16[2,128,1792]{2,1,0:T(8,128)(2,1)}, u32[]{:S(2)}, u32[]{:S(2)}) collective-permute-start(bf16[2,128,1792]{2,1,0:T(8,128)(2,1)S(1)} %copy-done.2), channel_id=1, source_target_pairs={{1,0},{2,1},{3,2},{5,4},{6,5},{7,6},{9,8},{10,9},{11,10},{13,12},{... | collective-permute-start | bytes 2752520 | tf_op jit(solution)/shard_map/ppermute | solution.py:554
  54.9 14.0 %collective-permute-start.1 = (bf16[2,128,1792]{2,1,0:T(8,128)(2,1)}, bf16[2,128,1792]{2,1,0:T(8,128)(2,1)}, u32[]{:S(2)}, u32[]{:S(2)}) collective-permute-start(bf16[2,128,1792]{2,1,0:T(8,128)(2,1)} %collective-permute-done.refs_2_), channel_id=1, source_target_pairs={{1,2},{2,3},{5,6},{6,7},{9,10},{10,11},{13,14},{14,15},{17,18},{18... | collective-permute-start | bytes 2752520 | tf_op jit(solution)/shard_map/ppermute | solution.py:553
  57.3 26.2 %collective-permute-start.4 = (bf16[2,128,1792]{2,1,0:T(8,128)(2,1)}, bf16[2,128,1792]{2,1,0:T(8,128)(2,1)}, u32[]{:S(2)}, u32[]{:S(2)}) collective-permute-start(bf16[2,128,1792]{2,1,0:T(8,128)(2,1)} %collective-permute-done.3.refs_5_), channel_id=1, source_target_pairs={{1,0},{2,1},{5,4},{6,5},{9,8},{10,9},{13,12},{14,13},{17,16},{18,1... | collective-permute-start | bytes 2752520 | tf_op jit(solution)/shard_map/ppermute | solution.py:554
  62.0 23.0 %collective-permute-start.9 = (bf16[2,2,152,512]{3,2,1,0:T(8,128)(2,1)}, bf16[2,2,152,512]{3,2,1,0:T(8,128)(2,1)}, u32[]{:S(2)}, u32[]{:S(2)}) collective-permute-start(bf16[2,2,152,512]{3,2,1,0:T(8,128)(2,1)} %select_bitcast_fusion), channel_id=1, source_target_pairs={{0,16},{4,20},{8,24},{12,28},{16,0},{20,4},{24,8},{28,12},{1,17},{... | collective-permute-start | bytes 1867784 | tf_op jit(solution)/shard_map/ppermute | solution.py:493
  63.7 21.3 %collective-permute-start.7 = (bf16[2,2,152,512]{3,2,1,0:T(8,128)(2,1)}, bf16[2,2,152,512]{3,2,1,0:T(8,128)(2,1)}, u32[]{:S(2)}, u32[]{:S(2)}) collective-permute-start(bf16[2,2,152,512]{3,2,1,0:T(8,128)(2,1)} %select_bitcast_fusion.1), channel_id=1, source_target_pairs={{0,8},{4,12},{8,0},{12,4},{16,24},{20,28},{24,16},{28,20},{1,9},{5... | collective-permute-start | bytes 1867784 | tf_op jit(solution)/shard_map/ppermute | solution.py:493
  68.9 30.1 %collective-permute-start.2 = (bf16[2,128,1792]{2,1,0:T(8,128)(2,1)}, bf16[2,128,1792]{2,1,0:T(8,128)(2,1)}, u32[]{:S(2)}, u32[]{:S(2)}) collective-permute-start(bf16[2,128,1792]{2,1,0:T(8,128)(2,1)} %collective-permute-done.1.refs_3_), channel_id=1, source_target_pairs={{2,3},{6,7},{10,11},{14,15},{18,19},{22,23},{26,27},{30,31}} | collective-permute-start | bytes 2752520 | tf_op jit(solution)/shard_map/ppermute | solution.py:553
  83.4 23.5 %collective-permute-start.5 = (bf16[2,128,1792]{2,1,0:T(8,128)(2,1)}, bf16[2,128,1792]{2,1,0:T(8,128)(2,1)}, u32[]{:S(2)}, u32[]{:S(2)}) collective-permute-start(bf16[2,128,1792]{2,1,0:T(8,128)(2,1)} %collective-permute-done.4.refs_6_), channel_id=1, source_target_pairs={{1,0},{5,4},{9,8},{13,12},{17,16},{21,20},{25,24},{29,28}} | collective-permute-start | bytes 2752520 | tf_op jit(solution)/shard_map/ppermute | solution.py:554
  121.3 22.1 %collective-permute-start.12 = (bf16[256,1792]{1,0:T(8,128)(2,1)S(1)}, bf16[256,1792]{1,0:T(8,128)(2,1)S(1)}, u32[]{:S(2)}, u32[]{:S(2)}) collective-permute-start(bf16[256,1792]{1,0:T(8,128)(2,1)S(1)} %get-tuple-element.22), channel_id=1, source_target_pairs={{0,1},{3,2},{4,5},{7,6},{8,9},{11,10},{12,13},{15,14},{16,17},{19,... | collective-permute-start | bytes 2752520 | tf_op jit(solution)/shard_map/ppermute | solution.py:442
  122.7 37.9 %collective-permute-start.11 = (bf16[256,1792]{1,0:T(8,128)(2,1)}, bf16[256,1792]{1,0:T(8,128)(2,1)}, u32[]{:S(2)}, u32[]{:S(2)}) collective-permute-start(bf16[256,1792]{1,0:T(8,128)(2,1)} %get-tuple-element.21), channel_id=1, source_target_pairs={{0,1},{3,2},{4,5},{7,6},{8,9},{11,10},{12,13},{15,14},{16,17},{19,... | collective-permute-start | bytes 2752520 | tf_op jit(solution)/shard_map/ppermute | solution.py:443
  144.6 16.0 %collective-permute-start.13 = (bf16[256,1792]{1,0:T(8,128)(2,1)}, bf16[256,1792]{1,0:T(8,128)(2,1)}, u32[]{:S(2)}, u32[]{:S(2)}) collective-permute-start(bf16[256,1792]{1,0:T(8,128)(2,1)} %add.150), channel_id=1, source_target_pairs={{1,2},{2,1},{5,6},{6,5},{9,10},{10,9},{13,14},{14,13},{17,18},{18,... | collective-permute-start | bytes 2752520 | tf_op jit(solution)/shard_map/ppermute | solution.py:444
  178.8 31.3 %collective-permute-start.18 = (bf16[256,1792]{1,0:T(8,128)(2,1)}, bf16[256,1792]{1,0:T(8,128)(2,1)}, u32[]{:S(2)}, u32[]{:S(2)}) collective-permute-start(bf16[256,1792]{1,0:T(8,128)(2,1)} %get-tuple-element.25), channel_id=1, source_target_pairs={{0,1},{3,2},{4,5},{7,6},{8,9},{11,10},{12,13},{15,14},{16,17},{19,... | collective-permute-start | bytes 2752520 | tf_op jit(solution)/shard_map/ppermute | solution.py:442
  208.5 15.5 %collective-permute-start.17 = (bf16[256,1792]{1,0:T(8,128)(2,1)S(1)}, bf16[256,1792]{1,0:T(8,128)(2,1)S(1)}, u32[]{:S(2)}, u32[]{:S(2)}) collective-permute-start(bf16[256,1792]{1,0:T(8,128)(2,1)S(1)} %copy-done.10), channel_id=1, source_target_pairs={{0,1},{3,2},{4,5},{7,6},{8,9},{11,10},{12,13},{15,14},{16,17},{19,... | collective-permute-start | bytes 2752520 | tf_op jit(solution)/shard_map/ppermute | solution.py:443
  212.8 25.2 %collective-permute-start.14 = (bf16[256,1792]{1,0:T(8,128)(2,1)S(1)}, bf16[256,1792]{1,0:T(8,128)(2,1)S(1)}, u32[]{:S(2)}, u32[]{:S(2)}) collective-permute-start(bf16[256,1792]{1,0:T(8,128)(2,1)S(1)} %copy-done.4), channel_id=1, source_target_pairs={{1,0},{2,3},{5,4},{6,7},{9,8},{10,11},{13,12},{14,15},{17,16},{18,... | collective-permute-start | bytes 2752520 | tf_op jit(solution)/shard_map/ppermute | solution.py:450
  214.1 36.4 %collective-permute-start.16 = (bf16[256,1792]{1,0:T(8,128)(2,1)S(1)}, bf16[256,1792]{1,0:T(8,128)(2,1)S(1)}, u32[]{:S(2)}, u32[]{:S(2)}) collective-permute-start(bf16[256,1792]{1,0:T(8,128)(2,1)S(1)} %collective-permute-done.15.refs_3_), channel_id=1, source_target_pairs={{1,0},{2,3},{5,4},{6,7},{9,8},{10,11},{13,12},{14,15},{17,16},{18,... | collective-permute-start | bytes 2752520 | tf_op jit(solution)/shard_map/ppermute | solution.py:451
  264.2 22.3 %collective-permute-start.21 = (bf16[256,1792]{1,0:T(8,128)(2,1)S(1)}, bf16[256,1792]{1,0:T(8,128)(2,1)S(1)}, u32[]{:S(2)}, u32[]{:S(2)}) collective-permute-start(bf16[256,1792]{1,0:T(8,128)(2,1)S(1)} %get-tuple-element.27), channel_id=1, source_target_pairs={{0,1},{3,2},{4,5},{7,6},{8,9},{11,10},{12,13},{15,14},{16,17},{19,... | collective-permute-start | bytes 2752520 | tf_op jit(solution)/shard_map/ppermute | solution.py:442
  265.7 23.0 %collective-permute-start.27 = (bf16[256,1792]{1,0:T(8,128)(2,1)S(1)}, bf16[256,1792]{1,0:T(8,128)(2,1)S(1)}, u32[]{:S(2)}, u32[]{:S(2)}) collective-permute-start(bf16[256,1792]{1,0:T(8,128)(2,1)S(1)} %add_convert_fusion.4.refs_9_.refs_1_), channel_id=1, source_target_pairs={{1,2},{2,1},{5,6},{6,5},{9,10},{10,9},{13,14},{14,13},{17,18},{18,... | collective-permute-start | bytes 2752520 | tf_op jit(solution)/shard_map/ppermute | solution.py:449
  266.5 31.7 %collective-permute-start.20 = (bf16[256,1792]{1,0:T(8,128)(2,1)S(1)}, bf16[256,1792]{1,0:T(8,128)(2,1)S(1)}, u32[]{:S(2)}, u32[]{:S(2)}) collective-permute-start(bf16[256,1792]{1,0:T(8,128)(2,1)S(1)} %get-tuple-element.26), channel_id=1, source_target_pairs={{0,1},{3,2},{4,5},{7,6},{8,9},{11,10},{12,13},{15,14},{16,17},{19,... | collective-permute-start | bytes 2752520 | tf_op jit(solution)/shard_map/ppermute | solution.py:443
  287.5 20.4 %collective-permute-start.26 = (bf16[256,1792]{1,0:T(8,128)(2,1)S(1)}, bf16[256,1792]{1,0:T(8,128)(2,1)S(1)}, u32[]{:S(2)}, u32[]{:S(2)}) collective-permute-start(bf16[256,1792]{1,0:T(8,128)(2,1)S(1)} %add_convert_fusion.4.refs_9_.refs_1_), channel_id=1, source_target_pairs={{1,0},{2,3},{5,4},{6,7},{9,8},{10,11},{13,12},{14,15},{17,16},{18,... | collective-permute-start | bytes 2752520 | tf_op jit(solution)/shard_map/ppermute | solution.py:450
  288.8 28.9 %collective-permute-start.28 = (bf16[256,1792]{1,0:T(8,128)(2,1)S(1)}, bf16[256,1792]{1,0:T(8,128)(2,1)S(1)}, u32[]{:S(2)}, u32[]{:S(2)}) collective-permute-start(bf16[256,1792]{1,0:T(8,128)(2,1)S(1)} %collective-permute-done.27.refs_3_), channel_id=1, source_target_pairs={{1,0},{2,3},{5,4},{6,7},{9,8},{10,11},{13,12},{14,15},{17,16},{18,... | collective-permute-start | bytes 2752520 | tf_op jit(solution)/shard_map/ppermute | solution.py:451
  331.7 13.9 %collective-permute-start.30 = (bf16[256,1792]{1,0:T(8,128)(2,1)S(1)}, bf16[256,1792]{1,0:T(8,128)(2,1)S(1)}, u32[]{:S(2)}, u32[]{:S(2)}) collective-permute-start(bf16[256,1792]{1,0:T(8,128)(2,1)S(1)} %get-tuple-element.29), channel_id=1, source_target_pairs={{0,1},{3,2},{4,5},{7,6},{8,9},{11,10},{12,13},{15,14},{16,17},{19,... | collective-permute-start | bytes 2752520 | tf_op jit(solution)/shard_map/ppermute | solution.py:442
  333.2 14.7 %collective-permute-start.24 = (bf16[256,1792]{1,0:T(8,128)(2,1)S(1)}, bf16[256,1792]{1,0:T(8,128)(2,1)S(1)}, u32[]{:S(2)}, u32[]{:S(2)}) collective-permute-start(bf16[256,1792]{1,0:T(8,128)(2,1)S(1)} %add_convert_fusion.3.refs_9_.own), channel_id=1, source_target_pairs={{1,2},{2,1},{5,6},{6,5},{9,10},{10,9},{13,14},{14,13},{17,18},{18,... | collective-permute-start | bytes 2752520 | tf_op jit(solution)/shard_map/ppermute | solution.py:449
  333.9 21.5 %collective-permute-start.29 = (bf16[256,1792]{1,0:T(8,128)(2,1)S(1)}, bf16[256,1792]{1,0:T(8,128)(2,1)S(1)}, u32[]{:S(2)}, u32[]{:S(2)}) collective-permute-start(bf16[256,1792]{1,0:T(8,128)(2,1)S(1)} %get-tuple-element.28), channel_id=1, source_target_pairs={{0,1},{3,2},{4,5},{7,6},{8,9},{11,10},{12,13},{15,14},{16,17},{19,... | collective-permute-start | bytes 2752520 | tf_op jit(solution)/shard_map/ppermute | solution.py:443
  346.6 17.8 %collective-permute-start.23 = (bf16[256,1792]{1,0:T(8,128)(2,1)S(1)}, bf16[256,1792]{1,0:T(8,128)(2,1)S(1)}, u32[]{:S(2)}, u32[]{:S(2)}) collective-permute-start(bf16[256,1792]{1,0:T(8,128)(2,1)S(1)} %add_convert_fusion.3.refs_9_.own), channel_id=1, source_target_pairs={{1,0},{2,3},{5,4},{6,7},{9,8},{10,11},{13,12},{14,15},{17,16},{18,... | collective-permute-start | bytes 2752520 | tf_op jit(solution)/shard_map/ppermute | solution.py:450
  347.9 26.3 %collective-permute-start.25 = (bf16[256,1792]{1,0:T(8,128)(2,1)S(1)}, bf16[256,1792]{1,0:T(8,128)(2,1)S(1)}, u32[]{:S(2)}, u32[]{:S(2)}) collective-permute-start(bf16[256,1792]{1,0:T(8,128)(2,1)S(1)} %collective-permute-done.24.other), channel_id=1, source_target_pairs={{1,0},{2,3},{5,4},{6,7},{9,8},{10,11},{13,12},{14,15},{17,16},{18,... | collective-permute-start | bytes 2752520 | tf_op jit(solution)/shard_map/ppermute | solution.py:451
  399.7 19.9 %collective-permute-start.32 = (bf16[256,1792]{1,0:T(8,128)(2,1)S(1)}, bf16[256,1792]{1,0:T(8,128)(2,1)S(1)}, u32[]{:S(2)}, u32[]{:S(2)}) collective-permute-start(bf16[256,1792]{1,0:T(8,128)(2,1)S(1)} %get-tuple-element.30), channel_id=1, source_target_pairs={{0,1},{3,2},{4,5},{7,6},{8,9},{11,10},{12,13},{15,14},{16,17},{19,... | collective-permute-start | bytes 2752520 | tf_op jit(solution)/shard_map/ppermute | solution.py:443
  410.8 16.9 %collective-permute-start.36 = (bf16[256,1792]{1,0:T(8,128)(2,1)S(1)}, bf16[256,1792]{1,0:T(8,128)(2,1)S(1)}, u32[]{:S(2)}, u32[]{:S(2)}) collective-permute-start(bf16[256,1792]{1,0:T(8,128)(2,1)S(1)} %add_convert_fusion.2.dep.own), channel_id=1, source_target_pairs={{1,0},{2,3},{5,4},{6,7},{9,8},{10,11},{13,12},{14,15},{17,16},{18,... | collective-permute-start | bytes 2752520 | tf_op jit(solution)/shard_map/ppermute | solution.py:450
  412.4 25.2 %collective-permute-start.38 = (bf16[256,1792]{1,0:T(8,128)(2,1)S(1)}, bf16[256,1792]{1,0:T(8,128)(2,1)S(1)}, u32[]{:S(2)}, u32[]{:S(2)}) collective-permute-start(bf16[256,1792]{1,0:T(8,128)(2,1)S(1)} %collective-permute-done.37.other), channel_id=1, source_target_pairs={{1,0},{2,3},{5,4},{6,7},{9,8},{10,11},{13,12},{14,15},{17,16},{18,... | collective-permute-start | bytes 2752520 | tf_op jit(solution)/shard_map/ppermute | solution.py:451
  462.4 29.5 %collective-permute-start.39 = (bf16[256,1792]{1,0:T(8,128)(2,1)S(1)}, bf16[256,1792]{1,0:T(8,128)(2,1)}, u32[]{:S(2)}, u32[]{:S(2)}) collective-permute-start(bf16[256,1792]{1,0:T(8,128)(2,1)S(1)} %get-tuple-element.32), channel_id=1, source_target_pairs={{0,1},{3,2},{4,5},{7,6},{8,9},{11,10},{12,13},{15,14},{16,17},{19,... | collective-permute-start | bytes 2752520 | tf_op jit(solution)/shard_map/ppermute | solution.py:443
  474.4 17.5 %collective-permute-start.41 = (bf16[256,1792]{1,0:T(8,128)(2,1)}, bf16[256,1792]{1,0:T(8,128)(2,1)}, u32[]{:S(2)}, u32[]{:S(2)}) collective-permute-start(bf16[256,1792]{1,0:T(8,128)(2,1)} %add.170), channel_id=1, source_target_pairs={{1,2},{2,1},{5,6},{6,5},{9,10},{10,9},{13,14},{14,13},{17,18},{18,... | collective-permute-start | bytes 2752520 | tf_op jit(solution)/shard_map/ppermute | solution.py:444
  476.9 14.0 %collective-permute-start.35 = (bf16[128,1792]{1,0:T(8,128)(2,1)}, bf16[128,1792]{1,0:T(8,128)(2,1)S(1)}, u32[]{:S(2)}, u32[]{:S(2)}) collective-permute-start(bf16[128,1792]{1,0:T(8,128)(2,1)} %broadcast_select_fusion.1), channel_id=1, source_target_pairs={{1,0},{2,3},{5,4},{6,7},{9,8},{10,11},{13,12},{14,15},{17,16},{18,... | collective-permute-start | bytes 1376264 | tf_op jit(solution)/shard_map/ppermute | solution.py:624
  (49 other events, 303.8 us)
